TPU v7x, 128 devices: a whole 4x4x4 slice. The times are simulated.
128 devices in a mesh: node: 32 (over z, y, core), head: 4 (over x).
Axes of the slice: x: 4, y: 4, z: 4, core: 2. Of those that a mesh axis runs over, the one named last changes fastest.
Arguments:
- queries: bfloat16 [8192, 8, 8, 128], P('node', None, 'head')
- keys: bfloat16 [8192, 8, 128], P('node', 'head')
- values: bfloat16 [8192, 8, 128], P('node', 'head'), may hold values from -6 to 6
- grad_out: bfloat16 [8192, 8, 8, 128], P('node', None, 'head'), may hold values from -6 to 6
- parents: int32 [32], replicated, may hold values from -1 to 0, as said below
- node_lengths: int32 [32], replicated, may hold values from 64 to 256
Outputs:
- attended: bfloat16 [8192, 8, 8, 128], P('node', None, 'head')
- grad_queries: bfloat16 [8192, 8, 8, 128], P('node', None, 'head')
- grad_keys: bfloat16 [8192, 8, 128], P('node', 'head')
- grad_values: bfloat16 [8192, 8, 128], P('node', 'head')
Inputs may be any that keep to these rules, and one draw needn't show every extreme that they name: `parents`: nodes on node-axis indices p with p % 4 == 0 are roots (-1); every other node has parent slot 0 (there is one node per index of the node axis), so a tree spans 4 consecutive indices of the node axis.
All inputs are finite; a program needn't handle non-finite values.
Results may differ from a plain program's by a relative error of at most 0.0067.
Values may be sent and summed in bfloat16 or wider, within the bound.
A program may use at most 128 MiB of HBM per device.

v0:
```python
import jax
import jax.numpy as jnp
from jax import lax
from jax.sharding import PartitionSpec as P

NODE_TOK = 256
LEVELS = 4


def from_behind(block, axis, distance):
    devices = range(lax.axis_size(axis))
    route = [(i - distance, i) for i in devices if i - distance in devices]
    return lax.ppermute(block, axis, route)


def attend_block(query_rows, key_rows, value_rows, grad_rows, allowed):
    logit_scale = query_rows.shape[-1] ** (-0.5)
    attention_logits = (
        jnp.einsum("qhgd,khd->hgqk", query_rows, key_rows, preferred_element_type=jnp.float32)
        * logit_scale
    )
    attention_logits = jnp.where(allowed[None, None], attention_logits, -jnp.inf)
    top_score = jnp.max(attention_logits, -1, keepdims=True)
    expo = jnp.exp(attention_logits - top_score)
    weights = expo / jnp.sum(expo, -1, keepdims=True)
    weight_reduced = weights.astype(jnp.bfloat16)
    attention_output = jnp.einsum(
        "hgqk,khd->qhgd", weight_reduced, value_rows, preferred_element_type=jnp.float32
    )
    weight_gradient = jnp.einsum(
        "qhgd,khd->hgqk", grad_rows, value_rows, preferred_element_type=jnp.float32
    )
    row_dot = jnp.transpose(
        jnp.sum(grad_rows.astype(jnp.float32) * attention_output, -1), (1, 2, 0)
    )[..., None]
    score_gradient = (weights * (weight_gradient - row_dot)).astype(jnp.bfloat16)
    query_gradient = (
        logit_scale
        * jnp.einsum("hgqk,khd->qhgd", score_gradient, key_rows, preferred_element_type=jnp.float32)
    ).astype(jnp.bfloat16)
    key_gradient = logit_scale * jnp.einsum(
        "hgqk,qhgd->khd", score_gradient, query_rows, preferred_element_type=jnp.float32
    )
    value_gradient = jnp.einsum(
        "hgqk,qhgd->khd", weight_reduced, grad_rows, preferred_element_type=jnp.float32
    )
    return (attention_output.astype(jnp.bfloat16), query_gradient, key_gradient, value_gradient)


def fetch_levels(local_pair):
    received = [local_pair]
    for distance in range(1, LEVELS):
        received.append(from_behind(local_pair, "node", distance))
    return received


def return_levels(partials):
    running = partials[0]
    for distance in range(1, LEVELS):
        running = running + from_behind(partials[distance], "node", -distance)
    return running


def shards(queries, keys, values, grad_out, parents, node_lengths):
    local_pair = jnp.stack([keys, values])
    wide_pair = lax.all_gather(local_pair, "head", axis=2, tiled=True)
    received = fetch_levels(wide_pair)
    token_count = queries.shape[0]
    node_count = token_count // NODE_TOK
    total_nodes = parents.shape[0]
    device = lax.axis_index("node")
    current = device * node_count + jnp.arange(node_count, dtype=jnp.int32)
    present = jnp.ones((node_count,), dtype=bool)
    slot_list = []
    present_list = []
    column_lengths = []
    own_slots = jnp.arange(node_count, dtype=jnp.int32)
    for distance in range(LEVELS):
        clipped = jnp.clip(current, 0, total_nodes - 1)
        slot_list.append(jnp.clip(current - (device - distance) * node_count, 0, node_count - 1))
        present_list.append(present)
        level_nodes = jnp.clip((device - distance) * node_count + own_slots, 0, total_nodes - 1)
        column_lengths.append(jnp.take(node_lengths, level_nodes))
        parent_slot = jnp.take(parents, clipped)
        present = present & (parent_slot >= 0)
        current = (device - distance - 1) * node_count + jnp.maximum(parent_slot, 0)
    pair_all = jnp.concatenate(received, axis=1)
    key_rows = pair_all[0]
    value_rows = pair_all[1]
    column_count = LEVELS * token_count
    column_ids = jnp.arange(column_count, dtype=jnp.int32)
    column_level = column_ids // token_count
    column_slot = column_ids % token_count // NODE_TOK
    column_tok = column_ids % NODE_TOK
    length_table = jnp.stack(column_lengths)
    column_length = jnp.zeros((column_count,), jnp.int32)
    for distance in range(LEVELS):
        hit = (column_level == distance) & (column_slot == 0)
        column_length = jnp.where(hit, length_table[distance, 0], column_length)
    column_open = column_tok < column_length
    block_rows = min(128, NODE_TOK)
    outputs = []
    query_grads = []
    key_total = None
    value_total = None
    wanted_slot = jnp.zeros((column_count,), jnp.int32)
    level_live = jnp.zeros((column_count,), bool)
    for distance in range(LEVELS):
        on_level = column_level == distance
        wanted_slot = jnp.where(on_level, slot_list[distance][0], wanted_slot)
        level_live = jnp.where(on_level, present_list[distance][0], level_live)
    column_ok = column_open & level_live & (column_slot == wanted_slot)
    for start in range(0, NODE_TOK, block_rows):
        row_tok = start + jnp.arange(block_rows, dtype=jnp.int32)
        allowed = column_ok[None, :] & (
            (column_level > 0)[None, :] | (column_tok[None, :] <= row_tok[:, None])
        )
        out_block, query_block, key_block, value_block = attend_block(
            queries[start : start + block_rows],
            key_rows,
            value_rows,
            grad_out[start : start + block_rows],
            allowed,
        )
        outputs.append(out_block)
        query_grads.append(query_block)
        key_total = key_block if key_total is None else key_total + key_block
        value_total = value_block if value_total is None else value_total + value_block
    attended = jnp.concatenate(outputs, 0)
    grad_q = jnp.concatenate(query_grads, 0)
    grads = jnp.stack([key_total, value_total]).reshape(
        2, LEVELS, token_count, key_total.shape[1], key_total.shape[2]
    )
    partials = [grads[:, distance] for distance in range(LEVELS)]
    summed = lax.psum_scatter(return_levels(partials), "head", scatter_dimension=2, tiled=True)
    return (attended, grad_q, summed[0].astype(jnp.bfloat16), summed[1].astype(jnp.bfloat16))


def solution(mesh):
    in_specs = (
        P("node", None, "head", None),
        P("node", "head", None),
        P("node", "head", None),
        P("node", None, "head", None),
        P(),
        P(),
    )
    out_specs = (
        P("node", None, "head", None),
        P("node", None, "head", None),
        P("node", "head", None),
        P("node", "head", None),
    )
    return jax.shard_map(shards, mesh=mesh, in_specs=in_specs, out_specs=out_specs, check_vma=False)
```

profile of v0, /device:TPU:1, one launch (start us, length us, event | category | flops | bytes accessed | tf_op | source)
XLA Modules:
  0.0 302.3 jit_solution(10571702827240008924)
XLA Ops:
  7.2 0.0 all-gather.2.cloned.1.call-start
  7.2 1.1 copy_bitcast_fusion.4
  8.3 0.7 pad_maximum_fusion.3
  9.0 0.0 all-gather.2.cloned.1.call-update
  9.1 0.0 reduce-scatter.2.cloned.1.call-start
  9.1 27.4 %all-gather.2.cloned.1.call-done = bf16[2,256,8,128]{3,1,2,0:T(8,128)(2,1)} async-done(((bf16[2,256,2,128]{3,1,2,0:T(8,128)(2,1)}), bf16[2,256,8,128]{3,1,2,0:T(8,128)(2,1)}) %all-gather.2.cloned.1.call-update) | async-done | bytes 1048592 | tf_op jit(solution)/shard_map/all_gather | solution.py:66
  36.5 4.6 %collective-permute-start = (bf16[2,256,8,128]{3,1,2,0:T(8,128)(2,1)}, bf16[2,256,8,128]{3,1,2,0:T(8,128)(2,1)}, u32[]{:S(2)}, u32[]{:S(2)}) collective-permute-start(bf16[2,256,8,128]{3,1,2,0:T(8,128)(2,1)} %all-gather.2.cloned.1.call-done), channel_id=1, source_target_pairs={{0,4},{4,8},{8,12},{12,16},{16,20},{20,24},{24,28},{28,32},{32,36}... | collective-permute-start | bytes 3145736 | tf_op jit(solution)/shard_map/ppermute | solution.py:13
  41.1 1.9 fusion.54
  43.0 1.2 dynamic-slice.18
  44.9 1.2 dynamic-slice.19
  46.8 1.2 dynamic-slice.20
  48.7 1.5 fusion.56
  52.7 4.1 %collective-permute-start.1 = (bf16[2,256,8,128]{3,1,2,0:T(8,128)(2,1)}, bf16[2,256,8,128]{3,1,2,0:T(8,128)(2,1)}, u32[]{:S(2)}, u32[]{:S(2)}) collective-permute-start(bf16[2,256,8,128]{3,1,2,0:T(8,128)(2,1)} %all-gather.2.cloned.1.call-done), channel_id=1, source_target_pairs={{0,8},{4,12},{8,16},{12,20},{16,24},{20,28},{24,32},{28,36},{32,40... | collective-permute-start | bytes 3145736 | tf_op jit(solution)/shard_map/ppermute | solution.py:13
  56.8 3.5 %collective-permute-start.2 = (bf16[2,256,8,128]{3,1,2,0:T(8,128)(2,1)}, bf16[2,256,8,128]{3,1,2,0:T(8,128)(2,1)}, u32[]{:S(2)}, u32[]{:S(2)}) collective-permute-start(bf16[2,256,8,128]{3,1,2,0:T(8,128)(2,1)} %all-gather.2.cloned.1.call-done), channel_id=1, source_target_pairs={{0,12},{4,16},{8,20},{12,24},{16,28},{20,32},{24,36},{28,40},{32,4... | collective-permute-start | bytes 3145736 | tf_op jit(solution)/shard_map/ppermute | solution.py:13
  60.2 1.2 copy.75
  61.4 1.2 copy.76
  62.6 1.6 fusion.30
  64.2 1.5 fusion.55
  65.7 1.5 constant_dynamic-update-slice_fusion.3
  67.2 1.4 constant_dynamic-update-slice_fusion.2
  68.6 10.4 %collective-permute-done.1 = bf16[2,256,8,128]{3,1,2,0:T(8,128)(2,1)} collective-permute-done((bf16[2,256,8,128]{3,1,2,0:T(8,128)(2,1)}, bf16[2,256,8,128]{3,1,2,0:T(8,128)(2,1)}, u32[]{:S(2)}, u32[]{:S(2)}) %collective-permute-start.1) | collective-permute-done | bytes 1048608 | tf_op jit(solution)/shard_map/ppermute | solution.py:13
  79.0 1.4 constant_dynamic-update-slice_fusion.1
  80.4 20.5 %collective-permute-done.2 = bf16[2,256,8,128]{3,1,2,0:T(8,128)(2,1)} collective-permute-done((bf16[2,256,8,128]{3,1,2,0:T(8,128)(2,1)}, bf16[2,256,8,128]{3,1,2,0:T(8,128)(2,1)}, u32[]{:S(2)}, u32[]{:S(2)}) %collective-permute-start.2) | collective-permute-done | bytes 1048608 | tf_op jit(solution)/shard_map/ppermute | solution.py:13
  100.9 1.4 constant_dynamic-update-slice_fusion
  102.3 1.3 fusion.24
  103.6 4.9 %fusion.57 = (f32[8,2,128]{2,1,0:T(2,128)S(1)}, f32[8,2,128,1024]{2,3,1,0:T(8,128)S(1)}) fusion(f32[8,1024,128,2]{2,1,3,0:T(8,128)S(1)} %fusion.24, pred[128,1024]{0,1:T(8,128)(4,1)} %get-tuple-element.103), kind=kOutput, calls=%fused_computation.113 | output fusion | flops 12583935 | bytes 16916480 | tf_op jit(solution)/shard_map/sub | solution.py:24
  108.5 1.0 fusion.15
  109.5 1.7 multiply_reduce_fusion.1
  111.2 1.3 fusion.59
  112.5 1.1 copy-done.8
  113.6 1.3 fusion.23
  114.8 7.0 %fusion.58 = (f32[8,2,128]{2,1,0:T(2,128)S(1)}, f32[8,2,128,1024]{2,3,1,0:T(8,128)}) fusion(f32[8,1024,128,2]{2,1,3,0:T(8,128)S(1)} %fusion.23, pred[128,1024]{0,1:T(8,128)(4,1)} %get-tuple-element.104), kind=kOutput, calls=%fused_computation.114 | output fusion | flops 12583935 | bytes 16916480 | tf_op jit(solution)/shard_map/sub | solution.py:24
  121.8 4.5 %fusion.16 = bf16[8,2,128,1024]{2,3,1,0:T(8,128)(2,1)S(1)} fusion(f32[8,2,128,1024]{2,3,1,0:T(8,128)} %get-tuple-element.112, f32[8,2,128]{2,1,0:T(2,128)S(1)} %get-tuple-element.111), kind=kLoop, calls=%fused_computation.32 | loop fusion | flops 4194304 | bytes 12591104 | tf_op jit(solution)/shard_map/convert_element_type | solution.py:26
  126.4 0.1 copy-done.11
  126.5 1.7 multiply_reduce_fusion
  128.3 0.6 copy-done.10
  128.9 4.2 %fusion.3 = bf16[8,2,128,1024]{2,3,1,0:T(8,128)(2,1)S(1)} fusion(f32[8,2,128]{2,1,0:T(2,128)S(1)} %bitcast.160, f32[8,2,128,1024]{2,3,1,0:T(8,128)} %get-tuple-element.112, f32[8,2,128]{2,1,0:T(2,128)S(1)} %get-tuple-element.111, bf16[128,8,2,128]{0,3,2,1:T(8,128)(2,1)S(1)} %copy-done.11, bf16[2,1024,8,128]{3,1,2,0:T(8,128)(2,1)S(1)} %copy-done.10), kind=kOutput, calls=%fused_computation.10 | convolution fusion | flops 545259520 | bytes 15220736 | tf_op jit(solution)/shard_map/qhgd,khd->hgqk/dot_general | solution.py:30
  133.2 1.3 bitcast_add_fusion
  134.4 0.1 copy-done.13
  134.6 3.2 %fusion.5 = bf16[8,2,128,1024]{2,3,1,0:T(8,128)(2,1)S(1)} fusion(f32[8,2,128]{2,1,0:T(2,128)S(1)} %bitcast.159, f32[8,2,128,1024]{2,3,1,0:T(8,128)S(1)} %get-tuple-element.110, f32[8,2,128]{2,1,0:T(2,128)S(1)} %get-tuple-element.109, bf16[128,8,2,128]{0,3,2,1:T(8,128)(2,1)S(1)} %copy-done.13, bf16[2,1024,8,128]{3,1,2,0:T(8,128)(2,1)} %copy-done.7), kind=kOutput, calls=%fused_computation.13 | convolution fusion | flops 545259520 | bytes 15220736 | tf_op jit(solution)/shard_map/qhgd,khd->hgqk/dot_general | solution.py:30
  137.8 1.3 fusion.33
  139.1 0.7 copy-done.1
  139.8 1.3 fusion.8
  141.1 0.7 fusion.18
  141.8 0.2 copy.103
  142.0 0.1 copy.101
  142.2 0.1 copy.102
  142.3 1.3 collective-permute-start.4
  143.6 1.3 collective-permute-start.5
  144.9 2.1 collective-permute-start.3
  147.1 44.5 %collective-permute-done.4 = f32[2,256,8,128]{3,1,0,2:T(8,128)S(1)} collective-permute-done((f32[2,256,8,128]{3,1,0,2:T(8,128)S(1)}, f32[2,256,8,128]{3,1,0,2:T(8,128)S(1)}, u32[]{:S(2)}, u32[]{:S(2)}) %collective-permute-start.4) | collective-permute-done | bytes 2097184 | tf_op jit(solution)/shard_map/ppermute | solution.py:13
  191.5 44.9 %collective-permute-done.3 = f32[2,256,8,128]{3,1,0,2:T(8,128)S(1)} collective-permute-done((f32[2,256,8,128]{3,1,0,2:T(8,128)S(1)}, f32[2,256,8,128]{3,1,0,2:T(8,128)S(1)}, u32[]{:S(2)}, u32[]{:S(2)}) %collective-permute-start.3) | collective-permute-done | bytes 2097184 | tf_op jit(solution)/shard_map/ppermute | solution.py:13
  236.5 1.9 fusion.22
  238.4 0.0 reduce-scatter.2.cloned.1.call-update
  238.4 4.4 %fusion.27 = bf16[128,8,2,128]{3,0,2,1:T(8,128)(2,1)S(1)} fusion(bf16[8,2,128,1024]{2,3,1,0:T(8,128)(2,1)} %copy-done, bf16[2,1024,8,128]{3,1,2,0:T(8,128)(2,1)} %copy-done.7), kind=kOutput, calls=%fused_computation.54 | convolution fusion | flops 537395200 | bytes 6815744 | tf_op jit(solution)/shard_map/hgqk,khd->qhgd/dot_general | solution.py:39
  242.9 3.2 %fusion.28 = bf16[128,8,2,128]{3,0,2,1:T(8,128)(2,1)S(1)} fusion(bf16[8,2,128,1024]{2,3,1,0:T(8,128)(2,1)S(1)} %copy-done.2, bf16[2,1024,8,128]{3,1,2,0:T(8,128)(2,1)} %copy-done.7), kind=kOutput, calls=%fused_computation.55 | convolution fusion | flops 537395200 | bytes 6815744 | tf_op jit(solution)/shard_map/hgqk,khd->qhgd/dot_general | solution.py:39
  246.0 0.1 pad_maximum_fusion.2
  246.1 2.0 copy.49
  248.2 0.1 pad_maximum_fusion.1
  248.3 2.1 copy.48
  250.4 42.4 %reduce-scatter.2.cloned.1.call-done = f32[2,256,2,128]{3,1,0,2:T(8,128)} async-done(((f32[2,256,8,128]{3,1,0,2:T(8,128)}), f32[2,256,2,128]{3,1,0,2:T(8,128)}) %reduce-scatter.2.cloned.1.call-update) | async-done | bytes 524304 | tf_op jit(solution)/shard_map/reduce_scatter | solution.py:135
  292.8 1.1 convert.4
  293.9 0.8 copy.51
  294.7 0.8 copy.50
  (35 shorter events, 0.1 us)
Async XLA Ops:
  7.2 57.0 %copy-start.14 = (bf16[256,8,2,128]{3,2,1,0:T(2,128)(2,1)S(1)}, bf16[256,8,2,128]{3,2,1,0:T(2,128)(2,1)}, u32[]{:S(2)}) copy-start(bf16[256,8,2,128]{3,2,1,0:T(2,128)(2,1)} %param.6) | copy-start | bytes 3145732
  7.2 29.3 %all-gather.2.cloned.1.call-start = ((), (), s32[]{:S(2)}) async-start(), calls=%async_computation.1 | async-start | bytes 1310720 | tf_op jit(solution)/shard_map/all_gather | solution.py:66
  9.1 283.7 %reduce-scatter.2.cloned.1.call-start = ((), (), s32[]{:S(2)}) async-start(), calls=%async_computation.2 | async-start | bytes 2621440 | tf_op jit(solution)/shard_map/reduce_scatter | solution.py:135
  36.5 30.7 %collective-permute-start = (bf16[2,256,8,128]{3,1,2,0:T(8,128)(2,1)}, bf16[2,256,8,128]{3,1,2,0:T(8,128)(2,1)}, u32[]{:S(2)}, u32[]{:S(2)}) collective-permute-start(bf16[2,256,8,128]{3,1,2,0:T(8,128)(2,1)} %all-gather.2.cloned.1.call-done), channel_id=1, source_target_pairs={{0,4},{4,8},{8,12},{12,16},{16,20},{20,24},{24,28},{28,32},{32,36}... | collective-permute-start | bytes 3145736 | tf_op jit(solution)/shard_map/ppermute | solution.py:13
  52.7 26.3 %collective-permute-start.1 = (bf16[2,256,8,128]{3,1,2,0:T(8,128)(2,1)}, bf16[2,256,8,128]{3,1,2,0:T(8,128)(2,1)}, u32[]{:S(2)}, u32[]{:S(2)}) collective-permute-start(bf16[2,256,8,128]{3,1,2,0:T(8,128)(2,1)} %all-gather.2.cloned.1.call-done), channel_id=1, source_target_pairs={{0,8},{4,12},{8,16},{12,20},{16,24},{20,28},{24,32},{28,36},{32,40... | collective-permute-start | bytes 3145736 | tf_op jit(solution)/shard_map/ppermute | solution.py:13
  56.8 44.1 %collective-permute-start.2 = (bf16[2,256,8,128]{3,1,2,0:T(8,128)(2,1)}, bf16[2,256,8,128]{3,1,2,0:T(8,128)(2,1)}, u32[]{:S(2)}, u32[]{:S(2)}) collective-permute-start(bf16[2,256,8,128]{3,1,2,0:T(8,128)(2,1)} %all-gather.2.cloned.1.call-done), channel_id=1, source_target_pairs={{0,12},{4,16},{8,20},{12,24},{16,28},{20,32},{24,36},{28,40},{32,4... | collective-permute-start | bytes 3145736 | tf_op jit(solution)/shard_map/ppermute | solution.py:13
  65.7 36.6 %copy-start.5 = (bf16[128,8,2,128]{3,2,1,0:T(2,128)(2,1)}, bf16[128,8,2,128]{3,2,1,0:T(2,128)(2,1)S(1)}, u32[]{:S(2)}) copy-start(bf16[128,8,2,128]{3,2,1,0:T(2,128)(2,1)S(1)} %get-tuple-element.99) | copy-start | bytes 1572868
  102.3 7.2 %copy-start.7 = (bf16[2,1024,8,128]{3,1,2,0:T(8,128)(2,1)}, bf16[2,1024,8,128]{3,1,2,0:T(8,128)(2,1)S(1)}, u32[]{:S(2)}) copy-start(bf16[2,1024,8,128]{3,1,2,0:T(8,128)(2,1)S(1)} %constant_dynamic-update-slice_fusion) | copy-start | bytes 12582916
  108.4 1.0 copy-start.12
  111.2 1.3 copy-start.3
  111.2 2.4 copy-start.8
  121.8 4.6 %copy-start.9 = (bf16[2,1024,8,128]{3,1,2,0:T(8,128)(2,1)S(1)}, bf16[2,1024,8,128]{3,1,2,0:T(8,128)(2,1)}, u32[]{:S(2)}) copy-start(bf16[2,1024,8,128]{3,1,2,0:T(8,128)(2,1)} %copy-done.7) | copy-start | bytes 12582916
  121.8 4.7 %copy-start.11 = (bf16[128,8,2,128]{0,3,2,1:T(8,128)(2,1)S(1)}, bf16[128,8,2,128]{0,3,2,1:T(8,128)(2,1)}, u32[]{:S(2)}) copy-start(bf16[128,8,2,128]{0,3,2,1:T(8,128)(2,1)} %copy.76) | copy-start | bytes 1572868
  126.5 2.4 copy-start.10
  133.2 6.0 %copy-start = (bf16[8,2,128,1024]{2,3,1,0:T(8,128)(2,1)}, bf16[8,2,128,1024]{2,3,1,0:T(8,128)(2,1)S(1)}, u32[]{:S(2)}) copy-start(bf16[8,2,128,1024]{2,3,1,0:T(8,128)(2,1)S(1)} %fusion.3) | copy-start | bytes 12582916
  133.2 1.4 copy-start.13
  134.6 3.2 %copy-start.6 = (bf16[128,8,2,128]{3,2,1,0:T(2,128)(2,1)S(1)}, bf16[128,8,2,128]{3,2,1,0:T(2,128)(2,1)}, u32[]{:S(2)}) copy-start(bf16[128,8,2,128]{3,2,1,0:T(2,128)(2,1)} %copy-done.5) | copy-start | bytes 1572868
  137.8 2.0 copy-start.1
  137.8 2.0 copy-start.4
  142.3 49.2 %collective-permute-start.4 = (f32[2,256,8,128]{3,1,0,2:T(8,128)S(1)}, f32[2,256,8,128]{3,1,0,2:T(8,128)S(1)}, u32[]{:S(2)}, u32[]{:S(2)}) collective-permute-start(f32[2,256,8,128]{3,1,0,2:T(8,128)S(1)} %bitcast.158), channel_id=1, source_target_pairs={{8,0},{12,4},{16,8},{20,12},{24,16},{28,20},{32,24},{36,28},{40,32... | collective-permute-start | bytes 6291464 | tf_op jit(solution)/shard_map/ppermute | solution.py:13
  143.6 47.9 %collective-permute-start.5 = (f32[2,256,8,128]{3,1,0,2:T(8,128)S(1)}, f32[2,256,8,128]{3,1,0,2:T(8,128)S(1)}, u32[]{:S(2)}, u32[]{:S(2)}) collective-permute-start(f32[2,256,8,128]{3,1,0,2:T(8,128)S(1)} %bitcast.157), channel_id=1, source_target_pairs={{12,0},{16,4},{20,8},{24,12},{28,16},{32,20},{36,24},{40,28},{44,3... | collective-permute-start | bytes 6291464 | tf_op jit(solution)/shard_map/ppermute | solution.py:13
  144.9 91.6 %collective-permute-start.3 = (f32[2,256,8,128]{3,1,0,2:T(8,128)S(1)}, f32[2,256,8,128]{3,1,0,2:T(8,128)S(1)}, u32[]{:S(2)}, u32[]{:S(2)}) collective-permute-start(f32[2,256,8,128]{3,1,0,2:T(8,128)S(1)} %bitcast.156), channel_id=1, source_target_pairs={{4,0},{8,4},{12,8},{16,12},{20,16},{24,20},{28,24},{32,28},{36,32}... | collective-permute-start | bytes 6291464 | tf_op jit(solution)/shard_map/ppermute | solution.py:13
  238.4 4.4 %copy-start.2 = (bf16[8,2,128,1024]{2,3,1,0:T(8,128)(2,1)S(1)}, bf16[8,2,128,1024]{2,3,1,0:T(8,128)(2,1)}, u32[]{:S(2)}) copy-start(bf16[8,2,128,1024]{2,3,1,0:T(8,128)(2,1)} %copy-done.1) | copy-start | bytes 12582916
  242.8 5.3 %copy-start.15 = (bf16[128,8,2,128]{0,3,2,1:T(8,128)(2,1)S(1)}, bf16[128,8,2,128]{0,3,2,1:T(8,128)(2,1)}, u32[]{:S(2)}) copy-start(bf16[128,8,2,128]{0,3,2,1:T(8,128)(2,1)} %get-tuple-element.94) | copy-start | bytes 1572868
  242.8 5.3 %copy-start.16 = (bf16[128,8,2,128]{0,3,2,1:T(8,128)(2,1)S(1)}, bf16[128,8,2,128]{0,3,2,1:T(8,128)(2,1)}, u32[]{:S(2)}) copy-start(bf16[128,8,2,128]{0,3,2,1:T(8,128)(2,1)} %get-tuple-element.98) | copy-start | bytes 1572868
Sparse Core Ops, SparseCore 0:
  10.2 26.2 all-gather.1
  238.6 54.1 reduce-scatter.1
where the time goes:
time: 303 us; the launch traced here: 302 us
  waiting for transfers between devices  190 us (63%)
  local copies, waits for them, and re-layouts  26.7 us (9%)
  matrix products  26 us (9%)
  other arithmetic  23.6 us (8%)
  between operations  18.9 us (6%)
  starting transfers between devices  16.9 us (6%)
    ppermute x6, waiting for transfers between devices, from_behind(): return lax.ppermute(block, axis, route)  120 us
    reduce_scatter x1, waiting for transfers between devices, shards(): lax.psum_scatter(return_levels(partials), 'head', scatter_dimension=2, ti...  42.4 us
    all_gather x1, waiting for transfers between devices, shards(): wide_pair = lax.all_gather(local_pair, 'head', axis=2, tiled=True)  27.4 us
    ppermute x6, starting transfers between devices, from_behind(): return lax.ppermute(block, axis, route)  16.9 us
    unnamed x46, local copies, waits for them, and re-layouts  15.5 us
    sub x2, other arithmetic, attend_block(): expo = jnp.exp(attention_logits - top_score)  11.9 us
    dot_general x2, matrix products, attend_block(): jnp.einsum('hgqk,khd->qhgd', score_gradient, key_rows, preferred_element_...  7.52 us
    dot_general x2, matrix products, attend_block(): jnp.einsum('qhgd,khd->hgqk', grad_rows, value_rows, preferred_element_typ...  7.45 us
  transfers between devices with their start and end apart: 8, of which 6 were waited for; matrix products, arithmetic and copies ran while one was open for 10% of the time, Pallas kernels for 0%

commit v1 on v0

v1 whole, which is shorter than its diff:
```python
import functools
import math

import jax
import jax.numpy as jnp
from jax import lax
from jax.experimental import pallas as pl
from jax.experimental.pallas import tpu as pltpu
from jax.sharding import PartitionSpec as P

MESH = pl.DeviceIdType.MESH
TOK = 256
LEVELS = 4
KVH = 8
HD = 128
ROWS = 512
SCALE = HD ** -0.5
SCORE_SCALE = SCALE * math.log2(math.e)

UNITS = ((0, 0), (1, 1), (3, 0), (2, 0), (2, 1), (1, 0), (3, 1), (0, 1))
ORDER = (0, 1, 2, 3, 4, 5, 6, 7)


def nt(a, b):
    return lax.dot_general(a, b, (((1,), (1,)), ((), ())), preferred_element_type=jnp.float32)


def tn(a, b):
    return lax.dot_general(a, b, (((0,), (0,)), ((), ())), preferred_element_type=jnp.float32)


def nn(a, b):
    return lax.dot_general(a, b, (((1,), (0,)), ((), ())), preferred_element_type=jnp.float32)


def when(cond, fn):
    if cond is None:
        fn()
    else:
        pl.when(cond)(fn)


def table(step, values):
    picked = jnp.int32(values[0])
    for at in range(1, len(values)):
        picked = jnp.where(step == at, jnp.int32(values[at]), picked)
    return picked


def kernel(
    q_ref, g_ref, k_ref, v_ref, len_ref,
    o_ref, dq_ref, dk_ref, dv_ref,
    kv, qh, gh, wide_o, wide_q, pair, score, part,
    sib_out, sib_in, x_out, x_in, transit, y_out, y_in,
    in_sem, out_sem, sib_sem, x_sem, transit_sem, y_sem,
):
    p = lax.axis_index("node")
    x = lax.axis_index("head")
    level = lax.rem(p, LEVELS)
    odd = lax.rem(p, 2)
    xp = lax.rem(x + 1, 4)
    xm = lax.rem(x + 3, 4)
    upper = level >= 2
    even = odd == 0
    to_xp = (p, xp)
    to_xm = (p, xm)
    to_sib = (p + 1 - 2 * odd, x)
    to_y = (p + 2 - 4 * (level // 2), x)

    def head_of(unit):
        hop, at = UNITS[unit]
        return 2 * lax.rem(x + hop, 4) + at

    sends = {}

    def define(name, cond, make):
        sends[name] = (cond, make, len(sends))

    def start(name):
        cond, make, at = sends[name]
        when(cond, lambda: make(at).start())

    def kv_copy(lev, head, unit, device):
        def make(at):
            return pltpu.make_async_remote_copy(
                src_ref=kv.at[lev, head], dst_ref=kv.at[lev, head],
                send_sem=out_sem.at[at], recv_sem=in_sem.at[lev, unit],
                device_id=device, device_id_type=MESH)
        return make

    def plain_copy(src, dst, sem, device):
        def make(at):
            return pltpu.make_async_remote_copy(
                src_ref=src, dst_ref=dst, send_sem=out_sem.at[at], recv_sem=sem,
                device_id=device, device_id_type=MESH)
        return make

    up2 = jnp.maximum(level - 2, 0)
    lev_of = (level, up2)
    cond_of = (None, upper)
    for a in range(2):
        lev, cond = lev_of[a], cond_of[a]
        define(("own", a, 1), cond, kv_copy(lev, head_of(7), 1, to_xm))
        define(("own", a, 2), cond, kv_copy(lev, head_of(0), 2, to_xp))
        define(("own", a, 5), cond, kv_copy(lev, head_of(0), 5, to_xm))
        define(("own", a, 6), cond, kv_copy(lev, head_of(7), 6, to_xp))
        define(("far", a, 3), cond, kv_copy(lev, head_of(2), 3, to_xp))
        define(("far", a, 4), cond, kv_copy(lev, head_of(1), 4, to_xm))
        for unit in range(8):
            define(("sib", a, unit), even if a == 0 else upper,
                   kv_copy(lev, head_of(unit), unit, to_sib))
    for unit in (0, 7):
        define(("up", unit), level < 2, kv_copy(level, head_of(unit), unit, to_y))
    for unit in range(8):
        define(("part", unit, 0), level >= 1,
               plain_copy(sib_out.at[unit, 0], sib_in.at[unit, 0], sib_sem.at[unit, 0], to_sib))
        define(("part", unit, 1), level == 3,
               plain_copy(sib_out.at[unit, 1], sib_in.at[unit, 1], sib_sem.at[unit, 1], to_sib))
    x_plan = {
        1: (to_xp, lambda a: (x_in.at[a, 1, 0], x_sem.at[a, 1, 0])),
        2: (to_xm, lambda a: (x_in.at[a, 0, 1], x_sem.at[a, 0, 1])),
        3: (to_xp, lambda a: (transit.at[a, 0], transit_sem.at[a, 0])),
        4: (to_xm, lambda a: (transit.at[a, 1], transit_sem.at[a, 1])),
        5: (to_xp, lambda a: (x_in.at[a, 0, 0], x_sem.at[a, 0, 0])),
        6: (to_xm, lambda a: (x_in.at[a, 1, 1], x_sem.at[a, 1, 1])),
    }
    for unit, (device, there) in x_plan.items():
        for a in range(2):
            dst, sem = there(a)
            define(("x", unit, a), cond_of[a], plain_copy(x_out.at[a, unit - 1], dst, sem, device))
    for at in range(2):
        define(("down", at), upper, plain_copy(y_out.at[at], y_in.at[at], y_sem.at[at], to_y))

    def wait_in(dst, sem):
        pltpu.make_async_remote_copy(
            src_ref=dst, dst_ref=dst, send_sem=out_sem.at[0], recv_sem=sem,
            device_id=to_sib, device_id_type=MESH).wait_recv()

    def wait_kv(lev, unit):
        wait_in(kv.at[lev, head_of(unit)], in_sem.at[lev, unit])

    def arrive(a, unit):
        def body():
            wait_kv(lev_of[a], unit)
            if a == 1 and unit == 0:
                start(("own", 1, 2))
                start(("own", 1, 5))
            if a == 1 and unit == 7:
                start(("own", 1, 1))
                start(("own", 1, 6))
            if unit == 2:
                start(("far", a, 3))
            if unit == 1:
                start(("far", a, 4))
            start(("sib", a, unit))
        when(cond_of[a], body)

    def from_sibling(unit):
        pl.when(level >= 1)(lambda: wait_kv(jnp.maximum(level - 1, 0), unit))
        pl.when(level == 3)(lambda: wait_kv(jnp.int32(0), unit))

    barrier = pltpu.get_barrier_semaphore()
    for device in (to_xp, to_xm, to_sib, to_y):
        pl.semaphore_signal(barrier, inc=1, device_id=device, device_id_type=MESH)

    for which, ref in ((0, k_ref), (1, v_ref)):
        pair[...] = ref[...].astype(jnp.float32)
        for at in range(2):
            kv[level, 2 * x + at, which] = pair[pl.ds(at, TOK, stride=2), :].astype(jnp.bfloat16)
    pl.semaphore_wait(barrier, 4)

    start(("own", 0, 1))
    start(("own", 0, 2))
    start(("up", 0))
    start(("up", 7))
    start(("sib", 0, 0))
    start(("sib", 0, 7))
    start(("own", 0, 5))
    start(("own", 0, 6))

    for lev in range(1, LEVELS):
        def blank(lev=lev):
            kv[lev] = jnp.zeros((KVH, 2, TOK, HD), jnp.bfloat16)
        pl.when(level < lev)(blank)

    for src, wide, dst in ((q_ref, wide_o, qh), (g_ref, wide_q, gh)):
        wide[...] = src[...].astype(jnp.float32)
        for head in range(KVH):
            for r in range(2):
                dst[head, r * TOK:(r + 1) * TOK, :] = (
                    wide[pl.ds(2 * head + r, TOK, stride=16), :].astype(jnp.bfloat16))

    lengths = []
    for k in range(LEVELS):
        real = len_ref[jnp.maximum(p - k, 0)]
        lengths.append(jnp.where(level >= k, real, 0))

    def compute(step):
        hop = table(step, [UNITS[u][0] for u in ORDER])
        at = table(step, [UNITS[u][1] for u in ORDER])
        unit = table(step, list(ORDER))
        head = 2 * lax.rem(x + hop, 4) + at
        q = qh[head]
        g = gh[head]
        levs = [lax.rem(level - k + LEVELS, LEVELS) for k in range(LEVELS)]
        key_row = lax.broadcasted_iota(jnp.int32, (TOK, ROWS), 0)
        query_tok = lax.rem(lax.broadcasted_iota(jnp.int32, (TOK, ROWS), 1), TOK)
        top = None
        for k in range(LEVELS):
            s = nt(kv[levs[k], head, 0], q) * SCORE_SCALE
            seen = key_row < lengths[k]
            if k == 0:
                seen = seen & (key_row <= query_tok)
            s = jnp.where(seen, s, -jnp.inf)
            score[k] = s
            high = jnp.max(s, axis=0, keepdims=True)
            top = high if top is None else jnp.maximum(top, high)
        total = None
        for k in range(LEVELS):
            e = jnp.exp2(score[k] - top)
            score[k] = e
            add = jnp.sum(e, axis=0, keepdims=True)
            total = add if total is None else total + add
        share = 1.0 / total
        out_t = None
        for k in range(LEVELS):
            w = score[k] * share
            score[k] = w
            low = w.astype(jnp.bfloat16)
            add = tn(kv[levs[k], head, 1], low)
            out_t = add if out_t is None else out_t + add
            dv = nn(low, g)
            if k % 2 == 0:
                part[unit, k // 2, 1] = dv
            else:
                sib_out[unit, k // 2, 1] = dv.astype(jnp.bfloat16)
        row_dot = jnp.sum(out_t * jnp.transpose(g.astype(jnp.float32)), axis=0, keepdims=True)
        dq_t = None
        for k in range(LEVELS):
            dw = nt(kv[levs[k], head, 1], g)
            ds = (score[k] * (dw - row_dot)).astype(jnp.bfloat16)
            add = tn(kv[levs[k], head, 0], ds)
            dq_t = add if dq_t is None else dq_t + add
            dk = nn(ds, q) * SCALE
            if k % 2 == 0:
                part[unit, k // 2, 0] = dk
            else:
                sib_out[unit, k // 2, 0] = dk.astype(jnp.bfloat16)
        out = jnp.transpose(out_t)
        dq = jnp.transpose(dq_t) * SCALE
        for r in range(2):
            wide_o[pl.ds(2 * head + r, TOK, stride=16), :] = out[r * TOK:(r + 1) * TOK]
            wide_q[pl.ds(2 * head + r, TOK, stride=16), :] = dq[r * TOK:(r + 1) * TOK]

    def add_sibling(unit):
        def first_even():
            wait_in(sib_in.at[unit, 0], sib_sem.at[unit, 0])
            part[unit, 0] = part[unit, 0] + sib_in[unit, 0].astype(jnp.float32)
        pl.when(even)(first_even)

        def first_last():
            wait_in(sib_in.at[unit, 0], sib_sem.at[unit, 0])
            part[unit, 1] = part[unit, 1] + sib_in[unit, 0].astype(jnp.float32)
        pl.when(level == 3)(first_last)

        def second():
            wait_in(sib_in.at[unit, 1], sib_sem.at[unit, 1])
            part[unit, 1] = part[unit, 1] + sib_in[unit, 1].astype(jnp.float32)
        pl.when(level == 2)(second)

    def finish(unit):
        add_sibling(unit)
        if unit in (0, 7):
            return
        for a in range(2):
            def body(a=a):
                got = part[unit, a]
                if unit in (5, 6):
                    wait_in(transit.at[a, unit - 5], transit_sem.at[a, unit - 5])
                    got = got + transit[a, unit - 5].astype(jnp.float32)
                x_out[a, unit - 1] = got.astype(jnp.bfloat16)
                start(("x", unit, a))
            when(cond_of[a], body)

    def gathered(a, at):
        for side in range(2):
            wait_in(x_in.at[a, at, side], x_sem.at[a, at, side])
        unit = 7 * at
        return (part[unit, a] + x_in[a, at, 0].astype(jnp.float32)
                + x_in[a, at, 1].astype(jnp.float32))

    def pass_down(at):
        def body():
            y_out[at] = gathered(1, at).astype(jnp.bfloat16)
            start(("down", at))
        pl.when(upper)(body)

    def before(unit):
        if unit == 0:
            arrive(1, 0)
            arrive(0, 1)
            arrive(0, 2)
        if unit == 1:
            arrive(1, 7)
            arrive(1, 2)
            arrive(1, 1)
        if unit == 2:
            arrive(0, 3)
            arrive(0, 4)
        if unit == 3:
            arrive(1, 3)
            arrive(0, 5)
        if unit == 4:
            arrive(1, 4)
            arrive(0, 6)
        if unit == 5:
            arrive(1, 5)
        if unit == 6:
            arrive(1, 6)
        from_sibling(unit)

    def after(unit):
        start(("part", unit, 0))
        start(("part", unit, 1))
        if unit > 0:
            finish(unit - 1)

    def step_body(step, carry):
        for at in range(8):
            pl.when(step == at)(functools.partial(before, ORDER[at]))
        compute(step)
        for at in range(8):
            pl.when(step == at)(functools.partial(after, ORDER[at]))
        return carry

    lax.fori_loop(0, 8, step_body, 0)
    pass_down(0)
    finish(7)
    pass_down(1)

    o_ref[...] = wide_o[...].astype(jnp.bfloat16)
    dq_ref[...] = wide_q[...].astype(jnp.bfloat16)

    for at in range(2):
        part[7 * at, 0] = gathered(0, at)

        def from_above(at=at):
            wait_in(y_in.at[at], y_sem.at[at])
            part[7 * at, 0] = part[7 * at, 0] + y_in[at].astype(jnp.float32)
        pl.when(level < 2)(from_above)
    for which, ref in ((0, dk_ref), (1, dv_ref)):
        for at in range(2):
            pair[pl.ds(at, TOK, stride=2), :] = part[7 * at, 0, which]
        ref[...] = pair[...].astype(jnp.bfloat16)

    for name, (cond, make, at) in sends.items():
        if name[0] == "sib" and name[1] == 1 or True:
            when(cond, lambda make=make, at=at: make(at).wait_send())


SENDS = 2 * (6 + 8) + 2 + 16 + 12 + 2


def shards(queries, keys, values, grad_out, parents, node_lengths):
    del parents
    tokens = queries.shape[0]
    wide_rows = tokens * KVH * 2
    vmem = pl.BlockSpec(memory_space=pltpu.VMEM)
    out = pl.pallas_call(
        kernel,
        out_shape=(
            jax.ShapeDtypeStruct((wide_rows, HD), jnp.bfloat16),
            jax.ShapeDtypeStruct((wide_rows, HD), jnp.bfloat16),
            jax.ShapeDtypeStruct((2 * tokens, HD), jnp.bfloat16),
            jax.ShapeDtypeStruct((2 * tokens, HD), jnp.bfloat16),
        ),
        in_specs=[vmem] * 4 + [pl.BlockSpec(memory_space=pltpu.SMEM)],
        out_specs=(vmem,) * 4,
        scratch_shapes=[
            pltpu.VMEM((LEVELS, KVH, 2, TOK, HD), jnp.bfloat16),
            pltpu.VMEM((KVH, ROWS, HD), jnp.bfloat16),
            pltpu.VMEM((KVH, ROWS, HD), jnp.bfloat16),
            pltpu.VMEM((wide_rows, HD), jnp.float32),
            pltpu.VMEM((wide_rows, HD), jnp.float32),
            pltpu.VMEM((2 * tokens, HD), jnp.float32),
            pltpu.VMEM((LEVELS, TOK, ROWS), jnp.float32),
            pltpu.VMEM((8, 2, 2, TOK, HD), jnp.float32),
            pltpu.VMEM((8, 2, 2, TOK, HD), jnp.bfloat16),
            pltpu.VMEM((8, 2, 2, TOK, HD), jnp.bfloat16),
            pltpu.VMEM((2, 6, 2, TOK, HD), jnp.bfloat16),
            pltpu.VMEM((2, 2, 2, 2, TOK, HD), jnp.bfloat16),
            pltpu.VMEM((2, 2, 2, TOK, HD), jnp.bfloat16),
            pltpu.VMEM((2, 2, TOK, HD), jnp.bfloat16),
            pltpu.VMEM((2, 2, TOK, HD), jnp.bfloat16),
            pltpu.SemaphoreType.DMA((LEVELS, 8)),
            pltpu.SemaphoreType.DMA((SENDS,)),
            pltpu.SemaphoreType.DMA((8, 2)),
            pltpu.SemaphoreType.DMA((2, 2, 2)),
            pltpu.SemaphoreType.DMA((2, 2)),
            pltpu.SemaphoreType.DMA((2,)),
        ],
        compiler_params=pltpu.CompilerParams(
            collective_id=0, has_side_effects=True, vmem_limit_bytes=48 * 1024 * 1024),
        cost_estimate=pl.CostEstimate(
            flops=12 * 16 * TOK * 4 * TOK * HD, bytes_accessed=5 * 1024 * 1024,
            transcendentals=16 * TOK * 4 * TOK),
    )(
        queries.reshape(wide_rows, HD),
        grad_out.reshape(wide_rows, HD),
        keys.reshape(2 * tokens, HD),
        values.reshape(2 * tokens, HD),
        node_lengths,
    )
    return (
        out[0].reshape(queries.shape),
        out[1].reshape(queries.shape),
        out[2].reshape(keys.shape),
        out[3].reshape(values.shape),
    )


def solution(mesh):
    in_specs = (
        P("node", None, "head", None),
        P("node", "head", None),
        P("node", "head", None),
        P("node", None, "head", None),
        P(),
        P(),
    )
    out_specs = (
        P("node", None, "head", None),
        P("node", None, "head", None),
        P("node", "head", None),
        P("node", "head", None),
    )
    return jax.shard_map(shards, mesh=mesh, in_specs=in_specs, out_specs=out_specs, check_vma=False)
```

time: 303 us -> 68.5 us (0.23)
  waiting for transfers between devices: 190 us -> 0 us
  Pallas kernels: 0 us -> 59.5 us
  matrix products: 26 us -> 0 us
  other arithmetic: 23.6 us -> 0 us
  local copies, waits for them, and re-layouts: 26.7 us -> 8.16 us
  between operations: 18.9 us -> 0.65 us
  starting transfers between devices: 16.9 us -> 0 us
    ppermute x6 -> x0, waiting for transfers between devices: 120 us -> none  [from_behind(): return lax.ppermute(block, axis, route)]
    pallas_call x0 -> x1, Pallas kernels: none -> 59.5 us  [shards(): pl.pallas_call(kernel, out_shape=(jax.ShapeDtypeStruct((wide_rows, HD), j...]
    reduce_scatter x1 -> x0, waiting for transfers between devices: 42.4 us -> none  [shards(): lax.psum_scatter(return_levels(partials), 'head', scatter_dimension=2, ti...]
    all_gather x1 -> x0, waiting for transfers between devices: 27.4 us -> none  [shards(): wide_pair = lax.all_gather(local_pair, 'head', axis=2, tiled=True)]
    dot_general x12 -> x0, matrix products: 26 us -> none  [the longest x2 7.52 us: attend_block(): jnp.einsum('hgqk,khd->qhgd', score_gradient, key_rows, preferred_element_...]
    ppermute x6 -> x0, starting transfers between devices: 16.9 us -> none  [from_behind(): return lax.ppermute(block, axis, route)]
    sub x2 -> x0, other arithmetic: 11.9 us -> none  [attend_block(): expo = jnp.exp(attention_logits - top_score)]
    unnamed x46 -> x14, local copies, waits for them, and re-layouts: 15.5 us -> 8.16 us
  transfers between devices with their start and end apart: 8 -> 0, of which waited for: 6 -> 0; matrix products, arithmetic and copies ran while one was open for 10% -> 0% of each run, Pallas kernels for 0% -> 0%
where the time goes in v1:
time: 68.5 us; the launch traced here: 68.3 us
  Pallas kernels  59.5 us (87%)
  local copies, waits for them, and re-layouts  8.16 us (12%)
    pallas_call x1, Pallas kernels, shards(): pl.pallas_call(kernel, out_shape=(jax.ShapeDtypeStruct((wide_rows, HD), j...  59.5 us
    unnamed x14, local copies, waits for them, and re-layouts  8.16 us

profile of v1, /device:TPU:1, one launch (start us, length us, event | category | flops | bytes accessed | tf_op | source)
XLA Modules:
  0.0 68.3 jit_solution(16953360057749868780)
XLA Ops:
  0.6 0.0 copy-start.4
  0.6 0.6 copy-done.4
  1.3 0.0 copy-start
  1.3 1.2 %copy-done = bf16[256,8,2,128]{3,2,1,0:T(2,128)(2,1)S(1)} copy-done((bf16[256,8,2,128]{3,2,1,0:T(2,128)(2,1)S(1)}, bf16[256,8,2,128]{3,2,1,0:T(2,128)(2,1)}, u32[]{:S(2)}) %copy-start) | copy-done | bytes 1048600
  2.5 0.0 copy-start.1
  2.5 1.2 %copy-done.1 = bf16[256,8,2,128]{3,2,1,0:T(2,128)(2,1)S(1)} copy-done((bf16[256,8,2,128]{3,2,1,0:T(2,128)(2,1)S(1)}, bf16[256,8,2,128]{3,2,1,0:T(2,128)(2,1)}, u32[]{:S(2)}) %copy-start.1) | copy-done | bytes 1048600
  3.7 0.0 copy-start.2
  3.7 0.9 %copy-done.2 = bf16[256,2,128]{2,1,0:T(2,128)(2,1)S(1)} copy-done((bf16[256,2,128]{2,1,0:T(2,128)(2,1)S(1)}, bf16[256,2,128]{2,1,0:T(2,128)(2,1)}, u32[]{:S(2)}) %copy-start.2) | copy-done | bytes 131096
  4.6 0.0 copy-start.3
  4.6 0.9 %copy-done.3 = bf16[256,2,128]{2,1,0:T(2,128)(2,1)S(1)} copy-done((bf16[256,2,128]{2,1,0:T(2,128)(2,1)S(1)}, bf16[256,2,128]{2,1,0:T(2,128)(2,1)}, u32[]{:S(2)}) %copy-start.3) | copy-done | bytes 131096
  5.5 59.5 %shard_map.84 = (bf16[4096,128]{1,0:T(8,128)(2,1)S(1)}, bf16[4096,128]{1,0:T(8,128)(2,1)S(1)}, bf16[512,128]{1,0:T(8,128)(2,1)S(1)}, bf16[512,128]{1,0:T(8,128)(2,1)S(1)}) custom-call(bf16[4096,128]{1,0:T(8,128)(2,1)S(1)} %bitcast.12, bf16[4096,128]{1,0:T(8,128)(2,1)S(1)} %bitcast.13, bf16[512,128]{1,0:T(8,128)(2,1)S(1)} %bitcast.14, ...), custom_call_target="tpu_custom_call" | custom-call | flops 6442450944 | bytes 5242880 | tf_op jit(solution)/shard_map/pallas_call | solution.py:369
  65.0 1.0 %copy.13 = bf16[256,8,2,128]{3,2,1,0:T(2,128)(2,1)} copy(bf16[256,8,2,128]{3,2,1,0:T(2,128)(2,1)S(1)} %bitcast.9) | data formatting | bytes 2097152
  66.0 1.0 %copy.14 = bf16[256,8,2,128]{3,2,1,0:T(2,128)(2,1)} copy(bf16[256,8,2,128]{3,2,1,0:T(2,128)(2,1)S(1)} %bitcast.8) | data formatting | bytes 2097152
  67.0 0.7 copy.15
  67.6 0.7 copy.16
Async XLA Ops:
  0.6 0.7 copy-start.4
  1.3 1.2 %copy-start = (bf16[256,8,2,128]{3,2,1,0:T(2,128)(2,1)S(1)}, bf16[256,8,2,128]{3,2,1,0:T(2,128)(2,1)}, u32[]{:S(2)}) copy-start(bf16[256,8,2,128]{3,2,1,0:T(2,128)(2,1)} %param.6) | copy-start | bytes 3145732
  2.5 1.2 %copy-start.1 = (bf16[256,8,2,128]{3,2,1,0:T(2,128)(2,1)S(1)}, bf16[256,8,2,128]{3,2,1,0:T(2,128)(2,1)}, u32[]{:S(2)}) copy-start(bf16[256,8,2,128]{3,2,1,0:T(2,128)(2,1)} %param.9) | copy-start | bytes 3145732
  3.7 0.9 %copy-start.2 = (bf16[256,2,128]{2,1,0:T(2,128)(2,1)S(1)}, bf16[256,2,128]{2,1,0:T(2,128)(2,1)}, u32[]{:S(2)}) copy-start(bf16[256,2,128]{2,1,0:T(2,128)(2,1)} %param.7) | copy-start | bytes 393220
  4.6 0.9 %copy-start.3 = (bf16[256,2,128]{2,1,0:T(2,128)(2,1)S(1)}, bf16[256,2,128]{2,1,0:T(2,128)(2,1)}, u32[]{:S(2)}) copy-start(bf16[256,2,128]{2,1,0:T(2,128)(2,1)} %param.8) | copy-start | bytes 393220

commit v2 on v0

v2 whole, which is shorter than its diff:
```python
import functools
import math

import jax
import jax.numpy as jnp
from jax import lax
from jax.experimental import pallas as pl
from jax.experimental.pallas import tpu as pltpu
from jax.sharding import PartitionSpec as P

MESH = pl.DeviceIdType.MESH
VMEM_BYTES = 63 * 1024 * 1024
UNLOADS = 2
TOK = 256
LEVELS = 4
KVH = 8
HD = 128
ROWS = 512
SCALE = HD ** -0.5
SCORE_SCALE = SCALE * math.log2(math.e)

STEPS = ((0, 0), (1, 0), (2, 0), (3, 1), (2, 1), (3, 0), (1, 1), (0, 1))
VIA_X = (2, 4)


def nt(a, b):
    return lax.dot_general(a, b, (((1,), (1,)), ((), ())), preferred_element_type=jnp.float32)


def tn(a, b):
    return lax.dot_general(a, b, (((0,), (0,)), ((), ())), preferred_element_type=jnp.float32)


def nn(a, b):
    return lax.dot_general(a, b, (((1,), (0,)), ((), ())), preferred_element_type=jnp.float32)


def table(step, values):
    picked = jnp.int32(values[0])
    for at in range(1, len(values)):
        picked = jnp.where(step == at, jnp.int32(values[at]), picked)
    return picked


def kernel(
    q_hbm, g_hbm, k_hbm, v_hbm, len_hbm,
    o_hbm, dq_hbm, dk_hbm, dv_hbm,
    q_rows, g_rows, k_rows, v_rows, lens,
    kv, qh, gh, wide_o, wide_q, pair, score, low, ds, part,
    sib_out, sib_in, x_out, x_in, y_out, y_in, x_out_up, x_in_up,
    load_sem, store_sem, in_sem, out_sem, sib_sem, x_sem, x_up_sem, y_sem,
):
    loads = [
        pltpu.make_async_copy(src, dst, load_sem.at[at])
        for at, (src, dst) in enumerate((
            (k_hbm, k_rows), (v_hbm, v_rows), (q_hbm, q_rows), (g_hbm, g_rows), (len_hbm, lens)))
    ]
    for load in loads:
        load.start()
    p = lax.axis_index("node")
    x = lax.axis_index("head")
    level = lax.rem(p, LEVELS)
    odd = lax.rem(p, 2)
    upper = level >= 2
    lower = level < 2
    even = odd == 0
    up2 = jnp.maximum(level - 2, 0)
    y_node = p + 2 - 4 * (level // 2)
    to_sib = (p + 1 - 2 * odd, x)
    to_y = (y_node, x)

    def along(distance):
        return lax.rem(x + distance + 4, 4)

    def hop_of(step):
        return table(step, [hop for hop, _ in STEPS])

    def head_of(step):
        return 2 * along(hop_of(step)) + table(step, [at for _, at in STEPS])

    def remote(src, dst, kind, step, sem, device):
        return pltpu.make_async_remote_copy(
            src_ref=src, dst_ref=dst, send_sem=out_sem.at[kind, step], recv_sem=sem,
            device_id=device, device_id_type=MESH)

    def own_x(step):
        slot = kv.at[level, 2 * x + table(step, [at for _, at in STEPS])]
        return remote(slot, slot, 0, step, in_sem.at[level, step], (p, along(-hop_of(step))))

    def up_copy(step):
        slot = kv.at[level, head_of(step)]
        return remote(slot, slot, 1, step, in_sem.at[level, step], to_y)

    def pass_x(step):
        hop, at = STEPS[step]
        slot = kv.at[up2, 2 * x + at]
        return remote(slot, slot, 2, step, in_sem.at[up2, step], (p, along(-hop)))

    def to_sibling(a, step):
        lev = up2 if a else level
        slot = kv.at[lev, head_of(step)]
        return remote(slot, slot, 3 + a, step, in_sem.at[lev, step], to_sib)

    def part_copy(n, step):
        return remote(sib_out.at[step, n], sib_in.at[step, n], 5 + n, step,
                      sib_sem.at[step, n], to_sib)

    def x_copy(step):
        return remote(x_out.at[step], x_in.at[step], 7, step, x_sem.at[step],
                      (p, along(hop_of(step))))

    def x_up_copy(step):
        hop, at = STEPS[step]
        return remote(x_out_up.at[at], x_in_up.at[at], 8, step, x_up_sem.at[at], (p, along(hop)))

    def down_copy(step):
        return remote(y_out.at[step], y_in.at[step], 9, step, y_sem.at[step], to_y)

    def wait_in(dst, sem):
        pltpu.make_async_remote_copy(
            src_ref=dst, dst_ref=dst, send_sem=out_sem.at[0, 0], recv_sem=sem,
            device_id=to_sib, device_id_type=MESH).wait_recv()

    def wait_kv(lev, step):
        wait_in(kv.at[lev, head_of(step)], in_sem.at[lev, step])

    def from_sibling(step):
        pl.when(level >= 1)(lambda: wait_kv(jnp.maximum(level - 1, 0), step))
        pl.when(level == 3)(lambda: wait_kv(jnp.int32(0), step))

    barrier = pltpu.get_barrier_semaphore()
    friends = [to_sib, to_y] + [(p, along(hop)) for hop in (1, 2, 3)]
    for device in friends:
        pl.semaphore_signal(barrier, inc=1, device_id=device, device_id_type=MESH)

    for which, ref in ((0, k_rows), (1, v_rows)):
        loads[which].wait()
        pair[...] = ref[...].astype(jnp.float32)
        for at in range(2):
            kv[level, 2 * x + at, which] = pair[pl.ds(at, TOK, stride=2), :].astype(jnp.bfloat16)
    pl.semaphore_wait(barrier, len(friends))

    def first_lower():
        up_copy(0).start()
        up_copy(7).start()

    def first_even():
        to_sibling(0, 0).start()
        to_sibling(0, 7).start()

    pl.when(even)(first_even)
    pl.when(lower)(first_lower)
    for step in (1, 3, 5, 6):
        own_x(step).start()

    def blank():
        kv[3] = jnp.zeros((KVH, 2, TOK, HD), jnp.bfloat16)
    pl.when(level == 0)(blank)

    for at, (src, wide, dst) in enumerate(((q_rows, wide_o, qh), (g_rows, wide_q, gh))):
        loads[2 + at].wait()
        wide[...] = src[...].astype(jnp.float32)
        for head in range(KVH):
            for r in range(2):
                dst[head, r * TOK:(r + 1) * TOK, :] = (
                    wide[pl.ds(2 * head + r, TOK, stride=16), :].astype(jnp.bfloat16))

    loads[4].wait()
    lengths = []
    for k in range(LEVELS):
        real = lens[jnp.maximum(p - k, 0)]
        lengths.append(jnp.where(level >= k, real, 0))

    def compute(step, blocks):
        head = head_of(step)
        q = qh[head]
        g = gh[head]
        levs = [lax.rem(level - k + LEVELS, LEVELS) for k in range(blocks)]
        key_row = lax.broadcasted_iota(jnp.int32, (TOK, TOK), 0)
        query_tok = lax.broadcasted_iota(jnp.int32, (TOK, TOK), 1)
        floor = jnp.finfo(jnp.float32).min
        keys = jnp.concatenate([kv[lev, head, 0] for lev in levs], axis=0)
        vals = jnp.concatenate([kv[lev, head, 1] for lev in levs], axis=0)
        half_q = [q[r * TOK:(r + 1) * TOK] for r in range(2)]
        half_g = [g[r * TOK:(r + 1) * TOK] for r in range(2)]

        def block(got, k):
            return got[k * TOK:(k + 1) * TOK]

        def softmax(r, scores):
            tops, sums = [], []
            for k in range(blocks):
                seen = key_row < lengths[k]
                if k == 0:
                    seen = seen & (key_row <= query_tok)
                one = jnp.where(seen, block(scores, k) * SCORE_SCALE, -jnp.inf)
                high = jnp.maximum(jnp.max(one, axis=0, keepdims=True), floor)
                expo = jnp.exp2(one - high)
                score[r, k] = expo
                tops.append(high)
                sums.append(jnp.sum(expo, axis=0, keepdims=True))
            top = functools.reduce(jnp.maximum, tops)
            fades = [jnp.exp2(high - top) for high in tops]
            share = 1.0 / sum(one * fade for one, fade in zip(sums, fades))
            factors = [fade * share for fade in fades]
            for k in range(blocks):
                low[r, k] = (score[r, k] * factors[k]).astype(jnp.bfloat16)
            return factors

        def attend(r):
            weights = low[r, 0:blocks].reshape(blocks * TOK, TOK)
            return tn(vals, weights), nn(weights, half_g[r])

        def score_grads(r, out, dw, factors):
            turned = jnp.transpose(half_g[r].astype(jnp.float32))
            row_dot = jnp.sum(out * turned, axis=0, keepdims=True)
            for k in range(blocks):
                slope = (block(dw, k) - row_dot) * factors[k]
                ds[r, k] = (score[r, k] * slope).astype(jnp.bfloat16)

        def back(r):
            slopes = ds[r, 0:blocks].reshape(blocks * TOK, TOK)
            return tn(keys, slopes), nn(slopes, half_q[r])

        def give(r, out, dq):
            wide_o[pl.ds(2 * head + r, TOK, stride=16), :] = jnp.transpose(out)
            wide_q[pl.ds(2 * head + r, TOK, stride=16), :] = jnp.transpose(dq) * SCALE

        factors0 = softmax(0, nt(keys, half_q[0]))
        scores1 = nt(keys, half_q[1])
        out0, dv0 = attend(0)
        factors1 = softmax(1, scores1)
        dw0 = nt(vals, half_g[0])
        out1, dv1 = attend(1)
        score_grads(0, out0, dw0, factors0)
        dw1 = nt(vals, half_g[1])
        dq0, dk0 = back(0)
        score_grads(1, out1, dw1, factors1)
        dq1, dk1 = back(1)
        give(0, out0, dq0)
        give(1, out1, dq1)
        for k in range(blocks):
            for which, got in ((1, block(dv0, k) + block(dv1, k)),
                               (0, (block(dk0, k) + block(dk1, k)) * SCALE)):
                if k % 2 == 0:
                    part[step, k // 2, which] = got
                else:
                    sib_out[step, k // 2, which] = got.astype(jnp.bfloat16)

    def add_sibling(step):
        def add(a, n):
            wait_in(sib_in.at[step, n], sib_sem.at[step, n])
            part[step, a] = part[step, a] + sib_in[step, n].astype(jnp.float32)
        pl.when(even)(lambda: add(0, 0))
        pl.when(level == 3)(lambda: add(1, 0))
        pl.when(level == 2)(lambda: add(1, 1))

    def send_x(step):
        x_out[step] = part[step, 0].astype(jnp.bfloat16)
        x_copy(step).start()

    def finish_upper(step):
        add_sibling(step)
        pl.when((step > 0) & (step < 7))(lambda: send_x(step))
        direct = (step > 0) & (step < 7)
        for via in VIA_X:
            def along_x(via=via):
                x_out_up[STEPS[via][1]] = part[via, 1].astype(jnp.bfloat16)
                x_up_copy(via).start()
            pl.when(step == via)(along_x)
            direct = direct & (step != via)
        pl.when(direct)(lambda: send_down(step))

    def send_down(step):
        y_out[step] = part[step, 1].astype(jnp.bfloat16)
        down_copy(step).start()

    def pass_down(at):
        wait_in(x_in_up.at[at], x_up_sem.at[at])
        part[7 * at, 1] = part[7 * at, 1] + x_in_up[at].astype(jnp.float32)
        send_down(7 * at)

    def add_down(step):
        wait_in(y_in.at[step], y_sem.at[step])
        part[step, 0] = part[step, 0] + y_in[step].astype(jnp.float32)

    def take_down(step):
        direct = step > 0
        for via in VIA_X:
            direct = direct & (step != via)
        pl.when(direct)(lambda: add_down(step))
        send_x(step)

    def arrive_same(step):
        def body():
            wait_kv(level, step)
            pl.when(even)(lambda: to_sibling(0, step).start())
        pl.when((step > 0) & (step < 7))(body)

    def arrive_upper(step):
        def below():
            wait_kv(up2, step)
            to_sibling(1, step).start()

        def last_early():
            wait_kv(up2, 7)
            pass_x(VIA_X[1]).start()
            to_sibling(1, 7).start()

        pl.when(step < 7)(below)
        pl.when(step == 0)(lambda: pass_x(VIA_X[0]).start())
        pl.when(step == 1)(last_early)
        arrive_same(step)

    def step_upper(step):
        pl.when(step < 2)(lambda: own_x(2 * step + 2).start())
        pl.when(step == 0)(lambda: arrive_upper(step))
        pl.when((step > 1) & (step < 7))(lambda: arrive_upper(step))
        pl.when(step > 0)(lambda: finish_upper(step - 1))
        pl.when(step == 6)(lambda: pass_down(0))
        from_sibling(step)
        pl.when(level == 3)(lambda: compute(step, 4))
        pl.when(level == 2)(lambda: compute(step, 3))
        part_copy(0, step).start()
        pl.when(level == 3)(lambda: part_copy(1, step).start())
        pl.when(step == 0)(lambda: arrive_upper(step + 1))

    def step_lower(step):
        pl.when(step < 2)(lambda: own_x(2 * step + 2).start())
        arrive_same(step)
        pl.when((step > 0) & (step < 7) & (step != VIA_X[0]) & (step != VIA_X[1]))(
            lambda: up_copy(step).start())
        pl.when((step > 0) & even)(lambda: add_sibling(step - 1))
        from_sibling(step)
        compute(step, 2)
        pl.when(level == 1)(lambda: part_copy(0, step).start())

    def step_body(step, carry):
        pl.when(upper)(lambda: step_upper(step))
        pl.when(lower)(lambda: step_lower(step))
        return carry

    lax.fori_loop(0, 8, step_body, 0)

    def last_upper():
        finish_upper(jnp.int32(7))
        pass_down(1)

    def last_lower():
        pl.when(even)(lambda: add_sibling(jnp.int32(7)))

        def down_body(step, carry):
            take_down(step)
            return carry
        lax.fori_loop(1, 7, down_body, 0)

    pl.when(upper)(last_upper)
    q_rows[...] = wide_o[...].astype(jnp.bfloat16)
    g_rows[...] = wide_q[...].astype(jnp.bfloat16)
    stores = [
        pltpu.make_async_copy(src, dst, store_sem.at[at])
        for at, (src, dst) in enumerate((
            (q_rows, o_hbm), (g_rows, dq_hbm), (k_rows, dk_hbm), (v_rows, dv_hbm)))
    ]
    stores[0].start()
    stores[1].start()
    pl.when(lower)(last_lower)

    for at in range(2):
        mine = 7 * at
        for step in range(1, 7):
            if STEPS[step][1] == at:
                wait_in(x_in.at[step], x_sem.at[step])
                part[mine, 0] = part[mine, 0] + x_in[step].astype(jnp.float32)
        pl.when(lower)(functools.partial(add_down, mine))
    for which, ref in ((0, k_rows), (1, v_rows)):
        for at in range(2):
            pair[pl.ds(at, TOK, stride=2), :] = part[7 * at, 0, which]
        ref[...] = pair[...].astype(jnp.bfloat16)
        stores[2 + which].start()

    for step in range(8):
        if 0 < step < 7:
            own_x(step).wait_send()
            x_copy(step).wait_send()
        if step in VIA_X:
            pl.when(upper)(lambda step=step: pass_x(step).wait_send())
            pl.when(upper)(lambda step=step: x_up_copy(step).wait_send())
        else:
            pl.when(lower)(lambda step=step: up_copy(step).wait_send())
            pl.when(upper)(lambda step=step: down_copy(step).wait_send())
        pl.when(even)(lambda step=step: to_sibling(0, step).wait_send())
        pl.when(upper)(lambda step=step: to_sibling(1, step).wait_send())
        pl.when(level >= 1)(lambda step=step: part_copy(0, step).wait_send())
        pl.when(level == 3)(lambda step=step: part_copy(1, step).wait_send())
    for store in stores:
        store.wait()


def unload(*refs):
    held, load_sem, store_sem = refs[8:12], refs[12], refs[13]
    moves = []
    for at in range(4):
        rows = refs[at].shape[0] // UNLOADS
        for piece in range(UNLOADS):
            cut = pl.ds(piece * rows, rows)
            moves.append((
                pltpu.make_async_copy(refs[at].at[cut], held[at].at[cut], load_sem.at[at, piece]),
                pltpu.make_async_copy(held[at].at[cut], refs[4 + at].at[cut], store_sem.at[at, piece])))
    for load, _ in moves:
        load.start()
    for load, store in moves:
        load.wait()
        store.start()
    for _, store in moves:
        store.wait()


def shards(queries, keys, values, grad_out, parents, node_lengths):
    del parents
    tokens = queries.shape[0]
    wide_rows = tokens * KVH * 2
    hbm = pl.BlockSpec(memory_space=pltpu.HBM)
    out = pl.pallas_call(
        kernel,
        out_shape=(
            jax.ShapeDtypeStruct((wide_rows, HD), jnp.bfloat16),
            jax.ShapeDtypeStruct((wide_rows, HD), jnp.bfloat16),
            jax.ShapeDtypeStruct((2 * tokens, HD), jnp.bfloat16),
            jax.ShapeDtypeStruct((2 * tokens, HD), jnp.bfloat16),
        ),
        in_specs=[hbm] * 5,
        out_specs=(hbm,) * 4,
        scratch_shapes=[
            pltpu.VMEM((wide_rows, HD), jnp.bfloat16),
            pltpu.VMEM((wide_rows, HD), jnp.bfloat16),
            pltpu.VMEM((2 * tokens, HD), jnp.bfloat16),
            pltpu.VMEM((2 * tokens, HD), jnp.bfloat16),
            pltpu.SMEM(node_lengths.shape, jnp.int32),
            pltpu.VMEM((LEVELS, KVH, 2, TOK, HD), jnp.bfloat16),
            pltpu.VMEM((KVH, ROWS, HD), jnp.bfloat16),
            pltpu.VMEM((KVH, ROWS, HD), jnp.bfloat16),
            pltpu.VMEM((wide_rows, HD), jnp.float32),
            pltpu.VMEM((wide_rows, HD), jnp.float32),
            pltpu.VMEM((2 * tokens, HD), jnp.float32),
            pltpu.VMEM((2, LEVELS, TOK, TOK), jnp.float32),
            pltpu.VMEM((2, LEVELS, TOK, TOK), jnp.bfloat16),
            pltpu.VMEM((2, LEVELS, TOK, TOK), jnp.bfloat16),
            pltpu.VMEM((8, 2, 2, TOK, HD), jnp.float32),
            pltpu.VMEM((8, 2, 2, TOK, HD), jnp.bfloat16),
            pltpu.VMEM((8, 2, 2, TOK, HD), jnp.bfloat16),
            pltpu.VMEM((8, 2, TOK, HD), jnp.bfloat16),
            pltpu.VMEM((8, 2, TOK, HD), jnp.bfloat16),
            pltpu.VMEM((8, 2, TOK, HD), jnp.bfloat16),
            pltpu.VMEM((8, 2, TOK, HD), jnp.bfloat16),
            pltpu.VMEM((2, 2, TOK, HD), jnp.bfloat16),
            pltpu.VMEM((2, 2, TOK, HD), jnp.bfloat16),
            pltpu.SemaphoreType.DMA((5,)),
            pltpu.SemaphoreType.DMA((4,)),
            pltpu.SemaphoreType.DMA((LEVELS, 8)),
            pltpu.SemaphoreType.DMA((10, 8)),
            pltpu.SemaphoreType.DMA((8, 2)),
            pltpu.SemaphoreType.DMA((8,)),
            pltpu.SemaphoreType.DMA((2,)),
            pltpu.SemaphoreType.DMA((8,)),
        ],
        compiler_params=pltpu.CompilerParams(
            collective_id=0, has_side_effects=True, vmem_limit_bytes=VMEM_BYTES),
        cost_estimate=pl.CostEstimate(
            flops=12 * 16 * TOK * 4 * TOK * HD, bytes_accessed=5 * 1024 * 1024,
            transcendentals=16 * TOK * 4 * TOK),
    )(
        queries.reshape(wide_rows, HD),
        grad_out.reshape(wide_rows, HD),
        keys.reshape(2 * tokens, HD),
        values.reshape(2 * tokens, HD),
        node_lengths,
    )
    out = pl.pallas_call(
        unload,
        out_shape=tuple(jax.ShapeDtypeStruct(one.shape, one.dtype) for one in out),
        in_specs=[hbm] * 4,
        out_specs=(hbm,) * 4,
        scratch_shapes=[pltpu.VMEM(one.shape, one.dtype) for one in out]
        + [pltpu.SemaphoreType.DMA((4, UNLOADS))] * 2,
        compiler_params=pltpu.CompilerParams(vmem_limit_bytes=VMEM_BYTES),
    )(*out)
    return (
        out[0].reshape(queries.shape),
        out[1].reshape(queries.shape),
        out[2].reshape(keys.shape),
        out[3].reshape(values.shape),
    )


def solution(mesh):
    in_specs = (
        P("node", None, "head", None),
        P("node", "head", None),
        P("node", "head", None),
        P("node", None, "head", None),
        P(),
        P(),
    )
    out_specs = (
        P("node", None, "head", None),
        P("node", None, "head", None),
        P("node", "head", None),
        P("node", "head", None),
    )
    return jax.shard_map(shards, mesh=mesh, in_specs=in_specs, out_specs=out_specs, check_vma=False)
```

time: 303 us -> 54.2 us (0.18)
  waiting for transfers between devices: 190 us -> 0 us
  Pallas kernels: 0 us -> 53.4 us
  local copies, waits for them, and re-layouts: 26.7 us -> 0 us
  matrix products: 26 us -> 0 us
  other arithmetic: 23.6 us -> 0 us
  between operations: 18.9 us -> 0.64 us
  starting transfers between devices: 16.9 us -> 0 us
    ppermute x6 -> x0, waiting for transfers between devices: 120 us -> none  [from_behind(): return lax.ppermute(block, axis, route)]
    pallas_call x0 -> x2, Pallas kernels: none -> 53.4 us  [the longest x1 50.8 us: shards(): pl.pallas_call(kernel, out_shape=(jax.ShapeDtypeStruct((wide_rows, HD), j...]
    reduce_scatter x1 -> x0, waiting for transfers between devices: 42.4 us -> none  [shards(): lax.psum_scatter(return_levels(partials), 'head', scatter_dimension=2, ti...]
    all_gather x1 -> x0, waiting for transfers between devices: 27.4 us -> none  [shards(): wide_pair = lax.all_gather(local_pair, 'head', axis=2, tiled=True)]
    dot_general x12 -> x0, matrix products: 26 us -> none  [the longest x2 7.52 us: attend_block(): jnp.einsum('hgqk,khd->qhgd', score_gradient, key_rows, preferred_element_...]
    ppermute x6 -> x0, starting transfers between devices: 16.9 us -> none  [from_behind(): return lax.ppermute(block, axis, route)]
    unnamed x46 -> x0, local copies, waits for them, and re-layouts: 15.5 us -> none
    sub x2 -> x0, other arithmetic: 11.9 us -> none  [attend_block(): expo = jnp.exp(attention_logits - top_score)]
  transfers between devices with their start and end apart: 8 -> 0, of which waited for: 6 -> 0; matrix products, arithmetic and copies ran while one was open for 10% -> 0% of each run, Pallas kernels for 0% -> 0%
where the time goes in v2:
time: 54.2 us; the launch traced here: 54 us
  Pallas kernels  53.4 us (99%)
  between operations  0.64 us (1%)
    pallas_call x1, Pallas kernels, shards(): pl.pallas_call(kernel, out_shape=(jax.ShapeDtypeStruct((wide_rows, HD), j...  50.8 us
    pallas_call x1, Pallas kernels, shards(): pl.pallas_call(unload, out_shape=tuple((jax.ShapeDtypeStruct(one.shape, o...  2.57 us

profile of v2, /device:TPU:1, one launch (start us, length us, event | category | flops | bytes accessed | tf_op | source)
XLA Modules:
  0.0 54.0 jit_solution(8496346074389327336)
XLA Ops:
  0.6 50.8 %shard_map.84 = (bf16[4096,128]{1,0:T(8,128)(2,1)}, bf16[4096,128]{1,0:T(8,128)(2,1)}, bf16[512,128]{1,0:T(8,128)(2,1)}, bf16[512,128]{1,0:T(8,128)(2,1)}) custom-call(bf16[4096,128]{1,0:T(8,128)(2,1)} %bitcast.8, bf16[4096,128]{1,0:T(8,128)(2,1)} %bitcast.9, bf16[512,128]{1,0:T(8,128)(2,1)} %bitcast.12, bf16[512,128]{1,0:T(8,128)(2,1)} %bitcast.13, s32[32]{0:T(128)} %len_hbm.1), custom_call_target="tpu_custom_call" | custom-call | flops 6442450944 | bytes 5242880 | tf_op jit(solution)/shard_map/pallas_call | solution.py:424
  51.5 2.6 %shard_map.85 = (bf16[4096,128]{1,0:T(8,128)(2,1)}, bf16[4096,128]{1,0:T(8,128)(2,1)}, bf16[512,128]{1,0:T(8,128)(2,1)}, bf16[512,128]{1,0:T(8,128)(2,1)}) custom-call(bf16[4096,128]{1,0:T(8,128)(2,1)} %get-tuple-element.12.refs_0_, bf16[4096,128]{1,0:T(8,128)(2,1)} %get-tuple-element.13.refs_1_, bf16[512,128]{1,0:T(8,128)(2,1)} %get-tuple-element.14.refs_2_, ...), custom_call_target="tpu_custom_call" | custom-call | tf_op jit(solution)/shard_map/pallas_call | solution.py:479

commit v3 on v2

--- a/solution.py
+++ b/solution.py
@@ -19,7 +19,7 @@
 SCALE = HD ** -0.5
 SCORE_SCALE = SCALE * math.log2(math.e)
 
-STEPS = ((0, 0), (1, 0), (2, 0), (3, 1), (2, 1), (3, 0), (1, 1), (0, 1))
+STEPS = ((0, 0), (1, 0), (3, 0), (3, 1), (1, 1), (2, 0), (2, 1), (0, 1))
 VIA_X = (2, 4)
 
 
@@ -150,7 +150,7 @@
 
     pl.when(even)(first_even)
     pl.when(lower)(first_lower)
-    for step in (1, 3, 5, 6):
+    for step in (1, 3, 2, 4):
         own_x(step).start()
 
     def blank():
@@ -313,9 +313,10 @@
         arrive_same(step)
 
     def step_upper(step):
-        pl.when(step < 2)(lambda: own_x(2 * step + 2).start())
+        pl.when(step < 2)(lambda: own_x(step + 5).start())
         pl.when(step == 0)(lambda: arrive_upper(step))
-        pl.when((step > 1) & (step < 7))(lambda: arrive_upper(step))
+        pl.when(step == 2)(lambda: arrive_upper(step))
+        pl.when((step > 1) & (step < 6))(lambda: arrive_upper(step + 1))
         pl.when(step > 0)(lambda: finish_upper(step - 1))
         pl.when(step == 6)(lambda: pass_down(0))
         from_sibling(step)
@@ -326,7 +327,7 @@
         pl.when(step == 0)(lambda: arrive_upper(step + 1))
 
     def step_lower(step):
-        pl.when(step < 2)(lambda: own_x(2 * step + 2).start())
+        pl.when(step < 2)(lambda: own_x(step + 5).start())
         arrive_same(step)
         pl.when((step > 0) & (step < 7) & (step != VIA_X[0]) & (step != VIA_X[1]))(
             lambda: up_copy(step).start())

time: 54.2 us -> 52.6 us (0.970)
  the two profiles are of different devices: /device:TPU:1 before, /device:TPU:103 now
where the time goes in v3:
time: 52.6 us; the launch traced here: 52.4 us
  Pallas kernels  51.8 us (98%)
  between operations  0.64 us (1%)
    pallas_call x1, Pallas kernels, shards(): pl.pallas_call(kernel, out_shape=(jax.ShapeDtypeStruct((wide_rows, HD), j...  49.2 us
    pallas_call x1, Pallas kernels, shards(): pl.pallas_call(unload, out_shape=tuple((jax.ShapeDtypeStruct(one.shape, o...  2.57 us

profile of v3, /device:TPU:103, one launch (start us, length us, event | category | flops | bytes accessed | tf_op | source)
XLA Modules:
  0.0 52.4 jit_solution(12454143450763676011)
XLA Ops:
  0.6 49.2 %shard_map.84 = (bf16[4096,128]{1,0:T(8,128)(2,1)}, bf16[4096,128]{1,0:T(8,128)(2,1)}, bf16[512,128]{1,0:T(8,128)(2,1)}, bf16[512,128]{1,0:T(8,128)(2,1)}) custom-call(bf16[4096,128]{1,0:T(8,128)(2,1)} %bitcast.8, bf16[4096,128]{1,0:T(8,128)(2,1)} %bitcast.9, bf16[512,128]{1,0:T(8,128)(2,1)} %bitcast.12, bf16[512,128]{1,0:T(8,128)(2,1)} %bitcast.13, s32[32]{0:T(128)} %len_hbm.1), custom_call_target="tpu_custom_call" | custom-call | flops 6442450944 | bytes 5242880 | tf_op jit(solution)/shard_map/pallas_call | solution.py:425
  49.9 2.6 %shard_map.85 = (bf16[4096,128]{1,0:T(8,128)(2,1)}, bf16[4096,128]{1,0:T(8,128)(2,1)}, bf16[512,128]{1,0:T(8,128)(2,1)}, bf16[512,128]{1,0:T(8,128)(2,1)}) custom-call(bf16[4096,128]{1,0:T(8,128)(2,1)} %get-tuple-element.12.refs_0_, bf16[4096,128]{1,0:T(8,128)(2,1)} %get-tuple-element.13.refs_1_, bf16[512,128]{1,0:T(8,128)(2,1)} %get-tuple-element.14.refs_2_, ...), custom_call_target="tpu_custom_call" | custom-call | tf_op jit(solution)/shard_map/pallas_call | solution.py:480

commit v4 on v3

--- a/solution.py
+++ b/solution.py
@@ -48,7 +48,7 @@
     q_rows, g_rows, k_rows, v_rows, lens,
     kv, qh, gh, wide_o, wide_q, pair, score, low, ds, part,
     sib_out, sib_in, x_out, x_in, y_out, y_in, x_out_up, x_in_up,
-    load_sem, store_sem, in_sem, out_sem, sib_sem, x_sem, x_up_sem, y_sem,
+    load_sem, store_sem, half_sem, in_sem, out_sem, sib_sem, x_sem, x_up_sem, y_sem,
 ):
     loads = [
         pltpu.make_async_copy(src, dst, load_sem.at[at])
@@ -91,6 +91,30 @@
         slot = kv.at[level, head_of(step)]
         return remote(slot, slot, 1, step, in_sem.at[level, step], to_y)
 
+    def own_half(which):
+        hop, at = STEPS[1]
+        slot = kv.at[level, 2 * x + at, which]
+        return remote(slot, slot, 0, 1 - which, half_sem.at[which], (p, along(-hop)))
+
+    def up_half(which):
+        slot = kv.at[level, head_of(1), which]
+        return remote(slot, slot, 1, 1 + which, in_sem.at[level, 1], to_y)
+
+    def arrive_halves():
+        for which in range(2):
+            wait_in(kv.at[level, head_of(1), which], half_sem.at[which])
+            up_half(which).start()
+        up_copy(7).start()
+        pl.when(even)(lambda: to_sibling(0, 1).start())
+
+    def down_half(which):
+        return remote(y_out.at[6, which], y_in.at[6, which], 9, 6 - 4 * which,
+                      y_sem.at[6 - 4 * which], to_y)
+
+    def x_half(which):
+        return remote(x_out.at[6, which], x_in.at[6, which], 7, 6 - 6 * which, x_sem.at[6],
+                      (p, along(STEPS[6][0])))
+
     def pass_x(step):
         hop, at = STEPS[step]
         slot = kv.at[up2, 2 * x + at]
@@ -142,7 +166,8 @@
 
     def first_lower():
         up_copy(0).start()
-        up_copy(7).start()
+        own_half(0).start()
+        own_half(1).start()
 
     def first_even():
         to_sibling(0, 0).start()
@@ -150,7 +175,8 @@
 
     pl.when(even)(first_even)
     pl.when(lower)(first_lower)
-    for step in (1, 3, 2, 4):
+    pl.when(upper)(lambda: own_x(1).start())
+    for step in (3, 2, 4):
         own_x(step).start()
 
     def blank():
@@ -261,8 +287,7 @@
 
     def finish_upper(step):
         add_sibling(step)
-        pl.when((step > 0) & (step < 7))(lambda: send_x(step))
-        direct = (step > 0) & (step < 7)
+        direct = (step > 0) & (step < 6)
         for via in VIA_X:
             def along_x(via=via):
                 x_out_up[STEPS[via][1]] = part[via, 1].astype(jnp.bfloat16)
@@ -271,6 +296,13 @@
             direct = direct & (step != via)
         pl.when(direct)(lambda: send_down(step))
 
+        def halves():
+            for which in range(2):
+                y_out[6, which] = part[6, 1, which].astype(jnp.bfloat16)
+                down_half(which).start()
+        pl.when(step == 6)(halves)
+        pl.when((step > 0) & (step < 7))(lambda: send_x(step))
+
     def send_down(step):
         y_out[step] = part[step, 1].astype(jnp.bfloat16)
         down_copy(step).start()
@@ -318,7 +350,7 @@
         pl.when(step == 2)(lambda: arrive_upper(step))
         pl.when((step > 1) & (step < 6))(lambda: arrive_upper(step + 1))
         pl.when(step > 0)(lambda: finish_upper(step - 1))
-        pl.when(step == 6)(lambda: pass_down(0))
+        pl.when(step == 5)(lambda: pass_down(0))
         from_sibling(step)
         pl.when(level == 3)(lambda: compute(step, 4))
         pl.when(level == 2)(lambda: compute(step, 3))
@@ -328,8 +360,9 @@
 
     def step_lower(step):
         pl.when(step < 2)(lambda: own_x(step + 5).start())
-        arrive_same(step)
-        pl.when((step > 0) & (step < 7) & (step != VIA_X[0]) & (step != VIA_X[1]))(
+        pl.when(step == 0)(arrive_halves)
+        pl.when(step > 1)(lambda: arrive_same(step))
+        pl.when((step > 1) & (step < 7) & (step != VIA_X[0]) & (step != VIA_X[1]))(
             lambda: up_copy(step).start())
         pl.when((step > 0) & even)(lambda: add_sibling(step - 1))
         from_sibling(step)
@@ -353,7 +386,12 @@
         def down_body(step, carry):
             take_down(step)
             return carry
-        lax.fori_loop(1, 7, down_body, 0)
+        lax.fori_loop(1, 6, down_body, 0)
+        for which in range(2):
+            wait_in(y_in.at[6, which], y_sem.at[6 - 4 * which])
+            x_out[6, which] = (
+                part[6, 0, which] + y_in[6, which].astype(jnp.float32)).astype(jnp.bfloat16)
+            x_half(which).start()
 
     pl.when(upper)(last_upper)
     q_rows[...] = wide_o[...].astype(jnp.bfloat16)
@@ -380,19 +418,38 @@
         ref[...] = pair[...].astype(jnp.bfloat16)
         stores[2 + which].start()
 
-    for step in range(8):
-        if 0 < step < 7:
+    def sent_upper():
+        for step in range(1, 7):
             own_x(step).wait_send()
             x_copy(step).wait_send()
-        if step in VIA_X:
-            pl.when(upper)(lambda step=step: pass_x(step).wait_send())
-            pl.when(upper)(lambda step=step: x_up_copy(step).wait_send())
-        else:
-            pl.when(lower)(lambda step=step: up_copy(step).wait_send())
-            pl.when(upper)(lambda step=step: down_copy(step).wait_send())
+        for step in range(8):
+            to_sibling(1, step).wait_send()
+            part_copy(0, step).wait_send()
+        for step in (0, 1, 3, 5, 7):
+            down_copy(step).wait_send()
+        for which in range(2):
+            down_half(which).wait_send()
+        for step in VIA_X:
+            pass_x(step).wait_send()
+            x_up_copy(step).wait_send()
+
+    def sent_lower():
+        for step in range(2, 7):
+            own_x(step).wait_send()
+        for step in range(1, 6):
+            x_copy(step).wait_send()
+        for which in range(2):
+            own_half(which).wait_send()
+            up_half(which).wait_send()
+            x_half(which).wait_send()
+        for step in (0, 3, 5, 6, 7):
+            up_copy(step).wait_send()
+
+    pl.when(upper)(sent_upper)
+    pl.when(lower)(sent_lower)
+    for step in range(8):
         pl.when(even)(lambda step=step: to_sibling(0, step).wait_send())
-        pl.when(upper)(lambda step=step: to_sibling(1, step).wait_send())
-        pl.when(level >= 1)(lambda step=step: part_copy(0, step).wait_send())
+        pl.when(level == 1)(lambda step=step: part_copy(0, step).wait_send())
         pl.when(level == 3)(lambda step=step: part_copy(1, step).wait_send())
     for store in stores:
         store.wait()
@@ -458,6 +515,7 @@
             pltpu.VMEM((2, 2, TOK, HD), jnp.bfloat16),
             pltpu.SemaphoreType.DMA((5,)),
             pltpu.SemaphoreType.DMA((4,)),
+            pltpu.SemaphoreType.DMA((2,)),
             pltpu.SemaphoreType.DMA((LEVELS, 8)),
             pltpu.SemaphoreType.DMA((10, 8)),
             pltpu.SemaphoreType.DMA((8, 2)),

time: 52.6 us -> 50 us (0.951)
  the two profiles are of different devices: /device:TPU:103 before, /device:TPU:1 now
where the time goes in v4:
time: 50 us; the launch traced here: 49.7 us
  Pallas kernels  49 us (98%)
  between operations  0.64 us (1%)
    pallas_call x1, Pallas kernels, shards(): pl.pallas_call(kernel, out_shape=(jax.ShapeDtypeStruct((wide_rows, HD), j...  46.5 us
    pallas_call x1, Pallas kernels, shards(): pl.pallas_call(unload, out_shape=tuple((jax.ShapeDtypeStruct(one.shape, o...  2.57 us

profile of v4, /device:TPU:1, one launch (start us, length us, event | category | flops | bytes accessed | tf_op | source)
XLA Modules:
  0.0 49.7 jit_solution(1666517223423443607)
XLA Ops:
  0.6 46.5 %shard_map.84 = (bf16[4096,128]{1,0:T(8,128)(2,1)}, bf16[4096,128]{1,0:T(8,128)(2,1)}, bf16[512,128]{1,0:T(8,128)(2,1)}, bf16[512,128]{1,0:T(8,128)(2,1)}) custom-call(bf16[4096,128]{1,0:T(8,128)(2,1)} %bitcast.8, bf16[4096,128]{1,0:T(8,128)(2,1)} %bitcast.9, bf16[512,128]{1,0:T(8,128)(2,1)} %bitcast.12, bf16[512,128]{1,0:T(8,128)(2,1)} %bitcast.13, s32[32]{0:T(128)} %len_hbm.1), custom_call_target="tpu_custom_call" | custom-call | flops 6442450944 | bytes 5242880 | tf_op jit(solution)/shard_map/pallas_call | solution.py:482
  47.1 2.6 %shard_map.85 = (bf16[4096,128]{1,0:T(8,128)(2,1)}, bf16[4096,128]{1,0:T(8,128)(2,1)}, bf16[512,128]{1,0:T(8,128)(2,1)}, bf16[512,128]{1,0:T(8,128)(2,1)}) custom-call(bf16[4096,128]{1,0:T(8,128)(2,1)} %get-tuple-element.12.refs_0_, bf16[4096,128]{1,0:T(8,128)(2,1)} %get-tuple-element.13.refs_1_, bf16[512,128]{1,0:T(8,128)(2,1)} %get-tuple-element.14.refs_2_, ...), custom_call_target="tpu_custom_call" | custom-call | tf_op jit(solution)/shard_map/pallas_call | solution.py:538

commit v5 on v4

--- a/solution.py
+++ b/solution.py
@@ -19,8 +19,10 @@
 SCALE = HD ** -0.5
 SCORE_SCALE = SCALE * math.log2(math.e)
 
-STEPS = ((0, 0), (1, 0), (3, 0), (3, 1), (1, 1), (2, 0), (2, 1), (0, 1))
+STEPS = ((0, 0), (1, 0), (3, 0), (2, 1), (1, 1), (2, 0), (3, 1), (0, 1))
 VIA_X = (2, 4)
+SEND_UPPER = ((2,), (4, 3), (6, 5))
+SEND_LOWER = ((2, 4), (3, 6), (5,))
 
 
 def nt(a, b):
@@ -176,8 +178,11 @@
     pl.when(even)(first_even)
     pl.when(lower)(first_lower)
     pl.when(upper)(lambda: own_x(1).start())
-    for step in (3, 2, 4):
-        own_x(step).start()
+    for cond, plan in ((upper, SEND_UPPER), (lower, SEND_LOWER)):
+        def send_first(plan=plan):
+            for step in plan[0]:
+                own_x(step).start()
+        pl.when(cond)(send_first)
 
     def blank():
         kv[3] = jnp.zeros((KVH, 2, TOK, HD), jnp.bfloat16)
@@ -344,8 +349,15 @@
         pl.when(step == 1)(last_early)
         arrive_same(step)
 
+    def send_own(step, plan):
+        for at, sent in enumerate(plan[1:]):
+            def go(sent=sent):
+                for one in sent:
+                    own_x(one).start()
+            pl.when(step == at)(go)
+
     def step_upper(step):
-        pl.when(step < 2)(lambda: own_x(step + 5).start())
+        send_own(step, SEND_UPPER)
         pl.when(step == 0)(lambda: arrive_upper(step))
         pl.when(step == 2)(lambda: arrive_upper(step))
         pl.when((step > 1) & (step < 6))(lambda: arrive_upper(step + 1))
@@ -359,7 +371,7 @@
         pl.when(step == 0)(lambda: arrive_upper(step + 1))
 
     def step_lower(step):
-        pl.when(step < 2)(lambda: own_x(step + 5).start())
+        send_own(step, SEND_LOWER)
         pl.when(step == 0)(arrive_halves)
         pl.when(step > 1)(lambda: arrive_same(step))
         pl.when((step > 1) & (step < 7) & (step != VIA_X[0]) & (step != VIA_X[1]))(

time: 50 us -> 49 us (0.980)
  Pallas kernels: 49 us -> 48.2 us
    pallas_call x1, Pallas kernels: 46.5 us -> 45.6 us  [shards(): pl.pallas_call(kernel, out_shape=(jax.ShapeDtypeStruct((wide_rows, HD), j...]
where the time goes in v5:
time: 49 us; the launch traced here: 48.8 us
  Pallas kernels  48.2 us (98%)
  between operations  0.64 us (1%)
    pallas_call x1, Pallas kernels, shards(): pl.pallas_call(kernel, out_shape=(jax.ShapeDtypeStruct((wide_rows, HD), j...  45.6 us
    pallas_call x1, Pallas kernels, shards(): pl.pallas_call(unload, out_shape=tuple((jax.ShapeDtypeStruct(one.shape, o...  2.57 us

profile of v5, /device:TPU:1, one launch (start us, length us, event | category | flops | bytes accessed | tf_op | source)
XLA Modules:
  0.0 48.8 jit_solution(17661994871725150626)
XLA Ops:
  0.6 45.6 %shard_map.84 = (bf16[4096,128]{1,0:T(8,128)(2,1)}, bf16[4096,128]{1,0:T(8,128)(2,1)}, bf16[512,128]{1,0:T(8,128)(2,1)}, bf16[512,128]{1,0:T(8,128)(2,1)}) custom-call(bf16[4096,128]{1,0:T(8,128)(2,1)} %bitcast.8, bf16[4096,128]{1,0:T(8,128)(2,1)} %bitcast.9, bf16[512,128]{1,0:T(8,128)(2,1)} %bitcast.12, bf16[512,128]{1,0:T(8,128)(2,1)} %bitcast.13, s32[32]{0:T(128)} %len_hbm.1), custom_call_target="tpu_custom_call" | custom-call | flops 6442450944 | bytes 5242880 | tf_op jit(solution)/shard_map/pallas_call | solution.py:494
  46.2 2.6 %shard_map.85 = (bf16[4096,128]{1,0:T(8,128)(2,1)}, bf16[4096,128]{1,0:T(8,128)(2,1)}, bf16[512,128]{1,0:T(8,128)(2,1)}, bf16[512,128]{1,0:T(8,128)(2,1)}) custom-call(bf16[4096,128]{1,0:T(8,128)(2,1)} %get-tuple-element.12.refs_0_, bf16[4096,128]{1,0:T(8,128)(2,1)} %get-tuple-element.13.refs_1_, bf16[512,128]{1,0:T(8,128)(2,1)} %get-tuple-element.14.refs_2_, ...), custom_call_target="tpu_custom_call" | custom-call | tf_op jit(solution)/shard_map/pallas_call | solution.py:550

commit v6 on v5

--- a/solution.py
+++ b/solution.py
@@ -22,7 +22,7 @@
 STEPS = ((0, 0), (1, 0), (3, 0), (2, 1), (1, 1), (2, 0), (3, 1), (0, 1))
 VIA_X = (2, 4)
 SEND_UPPER = ((2,), (4, 3), (6, 5))
-SEND_LOWER = ((2, 4), (3, 6), (5,))
+SEND_LOWER = ((2,), (3, 6), (5, 4))
 
 
 def nt(a, b):

time: 49 us -> 49.3 us (level); the launches traced: 48.8 us -> 48.5 us
  no operation moved by 1% of the time
where the time goes in v6:
time: 49.3 us; the launch traced here: 48.5 us
  Pallas kernels  47.9 us (97%)
  between operations  0.64 us (1%)
    pallas_call x1, Pallas kernels, shards(): pl.pallas_call(kernel, out_shape=(jax.ShapeDtypeStruct((wide_rows, HD), j...  45.3 us
    pallas_call x1, Pallas kernels, shards(): pl.pallas_call(unload, out_shape=tuple((jax.ShapeDtypeStruct(one.shape, o...  2.57 us

profile of v6, /device:TPU:1, one launch (start us, length us, event | category | flops | bytes accessed | tf_op | source)
XLA Modules:
  0.0 48.5 jit_solution(14360970937475867900)
XLA Ops:
  0.6 45.3 %shard_map.84 = (bf16[4096,128]{1,0:T(8,128)(2,1)}, bf16[4096,128]{1,0:T(8,128)(2,1)}, bf16[512,128]{1,0:T(8,128)(2,1)}, bf16[512,128]{1,0:T(8,128)(2,1)}) custom-call(bf16[4096,128]{1,0:T(8,128)(2,1)} %bitcast.8, bf16[4096,128]{1,0:T(8,128)(2,1)} %bitcast.9, bf16[512,128]{1,0:T(8,128)(2,1)} %bitcast.12, bf16[512,128]{1,0:T(8,128)(2,1)} %bitcast.13, s32[32]{0:T(128)} %len_hbm.1), custom_call_target="tpu_custom_call" | custom-call | flops 6442450944 | bytes 5242880 | tf_op jit(solution)/shard_map/pallas_call | solution.py:494
  46.0 2.6 %shard_map.85 = (bf16[4096,128]{1,0:T(8,128)(2,1)}, bf16[4096,128]{1,0:T(8,128)(2,1)}, bf16[512,128]{1,0:T(8,128)(2,1)}, bf16[512,128]{1,0:T(8,128)(2,1)}) custom-call(bf16[4096,128]{1,0:T(8,128)(2,1)} %get-tuple-element.12.refs_0_, bf16[4096,128]{1,0:T(8,128)(2,1)} %get-tuple-element.13.refs_1_, bf16[512,128]{1,0:T(8,128)(2,1)} %get-tuple-element.14.refs_2_, ...), custom_call_target="tpu_custom_call" | custom-call | tf_op jit(solution)/shard_map/pallas_call | solution.py:550
